TPU v7x, 32 devices: a whole 2x2x4 slice. The times are simulated.
32 devices in a mesh: section: 2 (over x), dp: 16 (over z, y, core).
Axes of the slice: x: 2, y: 2, z: 4, core: 2. Of those that a mesh axis runs over, the one named last changes fastest.
Arguments:
- incoming: bfloat16 [2, 4, 2048, 256], P('section', None, 'dp'), may hold values from -6 to 6
- feed: bfloat16 [4, 4, 2048, 256], P(None, None, 'dp'), may hold values from -6 to 6
- plan: int32 [1, 16], P(None, 'dp'), may hold values from 0 to 3, as said below
- weights: bfloat16 [2, 2, 27, 256, 256], P('section'), may hold values from -0.078125 to 0.078125
- momentum: float32 [2, 2, 27, 256, 256], P('section', None, None, 'dp'), may hold values from -6 to 6
Outputs:
- upstream: bfloat16 [2, 2, 4, 2048, 256], P(None, 'section', None, 'dp')
- new_momentum: float32 [2, 2, 27, 256, 256], P('section', None, None, 'dp')
Inputs may be any that keep to these rules, and one draw needn't show every extreme that they name: `plan`: every micro-batch of the pool is taken by some tile in some tick.
All inputs are finite; a program needn't handle non-finite values.
Results may differ from a plain program's by a relative error of at most 0.014.
Values may be sent and summed in bfloat16 or wider, within the bound.
A program may use at most 128 MiB of HBM per device.

v0:
```python
import jax
import jax.numpy as jnp
from jax import lax
from jax.sharding import PartitionSpec as P

TD = 2
TH = 8
TW = 8
TICKS = 2


def shifted(array, axis, by):
    size = lax.axis_size(axis)
    pairs = [(i, i + by) for i in range(size) if 0 <= i + by < size]
    return lax.ppermute(array, axis, pairs)


def make_patches(act, sign):
    channels = act.shape[-1]
    volume = act.reshape(TD, TH, TW, channels)
    padded = jnp.pad(volume, ((1, 1), (1, 1), (1, 1), (0, 0)))
    pieces = []
    for depth in (-1, 0, 1):
        for height in (-1, 0, 1):
            for width in (-1, 0, 1):
                start_d = 1 + sign * depth
                start_h = 1 + sign * height
                start_w = 1 + sign * width
                cut = padded[start_d : start_d + TD, start_h : start_h + TH, start_w : start_w + TW]
                pieces.append(cut.reshape(-1, channels))
    return jnp.stack(pieces, axis=1)


def silu_grad(value):
    sig = jax.nn.sigmoid(value)
    return sig * (1.0 + value * (1.0 - sig))


def half_g(inputs, weight_g):
    y_one = inputs[0]
    y_two = inputs[1]
    dy_one = inputs[2]
    dy_two = inputs[3]
    y_one_f = y_one.astype(jnp.float32)
    act_one = jax.nn.silu(y_one_f).astype(jnp.bfloat16)
    patch_one = make_patches(act_one, 1)
    g_out = jnp.einsum("vtc,toc->vo", patch_one, weight_g, preferred_element_type=jnp.float32)
    x_two = (y_two.astype(jnp.float32) - g_out).astype(jnp.bfloat16)
    grad_g = jnp.einsum("vo,vti->oti", dy_two, patch_one, preferred_element_type=jnp.float32)
    back_two = make_patches(dy_two, -1)
    d_act_one = jnp.einsum("vto,toi->vi", back_two, weight_g, preferred_element_type=jnp.float32)
    dx_one = (dy_one.astype(jnp.float32) + d_act_one * silu_grad(y_one_f)).astype(jnp.bfloat16)
    return (x_two, dx_one, grad_g)


def half_f(inputs, x_two, dx_one, weight_f):
    y_one_f = inputs[0].astype(jnp.float32)
    dy_two = inputs[3]
    x_two_f = x_two.astype(jnp.float32)
    act_two = jax.nn.silu(x_two_f).astype(jnp.bfloat16)
    patch_two = make_patches(act_two, 1)
    f_out = jnp.einsum("vtc,toc->vo", patch_two, weight_f, preferred_element_type=jnp.float32)
    x_one = (y_one_f - f_out).astype(jnp.bfloat16)
    grad_f = jnp.einsum("vo,vti->oti", dx_one, patch_two, preferred_element_type=jnp.float32)
    back_one = make_patches(dx_one, -1)
    d_act_two = jnp.einsum("vto,toi->vi", back_one, weight_f, preferred_element_type=jnp.float32)
    dx_two = (dy_two.astype(jnp.float32) + d_act_two * silu_grad(x_two_f)).astype(jnp.bfloat16)
    return (x_one, dx_two, grad_f)


def body(incoming, feed, plan, weights, momentum):
    replicas = lax.axis_size("dp")
    is_last = lax.axis_index("section") == lax.axis_size("section") - 1
    weight = weights[0]
    current = incoming[0]
    results = []
    out_channels = weight.shape[2]
    in_channels = weight.shape[3]
    total_f = jnp.zeros((out_channels, 27, in_channels), jnp.float32)
    total_g = jnp.zeros((out_channels, 27, in_channels), jnp.float32)
    for tick in range(TICKS):
        x_two, dx_one, grad_g = half_g(current, weight[1])
        total_g = total_g + grad_g
        x_one, dx_two, grad_f = half_f(current, x_two, dx_one, weight[0])
        total_f = total_f + grad_f
        outs = jnp.stack([x_one, x_two, dx_one, dx_two])
        results.append(outs)
        if tick + 1 < TICKS:
            from_below = shifted(outs, "section", -1)
            chosen = lax.dynamic_index_in_dim(feed, plan[tick, 0], 0, keepdims=False)
            current = jnp.where(is_last, chosen, from_below)
    both = jnp.stack([total_f, total_g], axis=1).astype(jnp.bfloat16).astype(jnp.float32)
    shard_rows = lax.psum_scatter(
        both.astype(jnp.bfloat16), "dp", scatter_dimension=0, tiled=True
    ).astype(jnp.float32)
    shard_total = jnp.transpose(shard_rows, (1, 2, 0, 3))
    upstream = jnp.stack(results)[:, None]
    new_momentum = 0.9 * momentum[0] + shard_total / (replicas * TICKS)
    return (upstream, new_momentum[None])


def solution(mesh):
    in_specs = (
        P("section", None, "dp", None),
        P(None, None, "dp", None),
        P(None, "dp"),
        P("section", None, None, None, None),
        P("section", None, None, "dp", None),
    )
    out_specs = (P(None, "section", None, "dp", None), P("section", None, None, "dp", None))
    return jax.shard_map(body, mesh=mesh, in_specs=in_specs, out_specs=out_specs, check_vma=False)
```

profile of v0, /device:TPU:0, one launch (start us, length us, event | category | flops | bytes accessed | tf_op | source)
XLA Modules:
  0.0 140.2 jit_solution(16105700549355156141)
XLA Ops:
  7.2 0.9 slice_convert_fusion.1
  8.9 0.7 copy-done.1
  9.8 1.4 copy-done.2
  11.2 1.3 fusion.106
  12.8 0.6 fusion.81
  14.0 0.6 fusion.96
  15.1 1.3 fusion.99
  16.4 1.5 %collective-permute-start = (bf16[4,128,256]{2,1,0:T(8,128)(2,1)S(1)}, bf16[4,128,256]{2,1,0:T(8,128)(2,1)S(1)}, u32[]{:S(2)}, u32[]{:S(2)}) collective-permute-start(bf16[4,128,256]{2,1,0:T(8,128)(2,1)S(1)} %get-tuple-element.7), channel_id=1, source_target_pairs={{16,0},{17,1},{18,2},{19,3},{20,4},{21,5},{22,6},{23,7},{24,8},{25... | collective-permute-start | bytes 786440 | tf_op jit(solution)/shard_map/ppermute | solution.py:15
  17.9 4.0 %fusion.146 = f32[256,27,256]{2,0,1:T(8,128)} fusion(bf16[128,27,256]{2,0,1:T(8,128)(2,1)S(1)} %constant_dynamic-update-slice_fusion.27, bf16[128,256]{1,0:T(8,128)(2,1)S(1)} %fusion.81), kind=kOutput, calls=%fused_computation.543 | convolution fusion | flops 452984832 | bytes 8912896 | tf_op jit(solution)/shard_map/vo,vti->oti/dot_general | solution.py:64
  22.6 1.1 fusion.143
  23.7 3.3 %collective-permute-done = bf16[4,128,256]{2,1,0:T(8,128)(2,1)S(1)} collective-permute-done((bf16[4,128,256]{2,1,0:T(8,128)(2,1)S(1)}, bf16[4,128,256]{2,1,0:T(8,128)(2,1)S(1)}, u32[]{:S(2)}, u32[]{:S(2)}) %collective-permute-start) | collective-permute-done | bytes 262176 | tf_op jit(solution)/shard_map/ppermute | solution.py:15
  27.0 1.0 bitcast_select_fusion
  29.0 0.8 slice-done.3
  29.8 1.3 fusion.112
  31.5 0.6 fusion.115
  32.1 1.1 fusion.2
  34.3 0.9 slice-done.1
  35.2 1.1 fusion.1
  36.4 3.5 %pad_maximum_fusion = bf16[256,2,27,256]{3,0,2,1:T(8,128)(2,1)} fusion(bf16[256,1,27,256]{3,0,2,1:T(8,128)(2,1)S(1)} %fusion.2, bf16[256,1,27,256]{3,0,2,1:T(8,128)(2,1)S(1)} %fusion.1), kind=kLoop, calls=%fused_computation | loop fusion | flops 3538944 | bytes 14155776 | tf_op jit(solution)/shard_map/stack | solution.py:92
  40.4 3.3 %fusion.93 = bf16[1,128,256]{2,1,0:T(8,128)(2,1)S(1)} fusion(bf16[128,27,256]{2,0,1:T(8,128)(2,1)S(1)} %constant_dynamic-update-slice_fusion.135, bf16[1,2,27,256,256]{4,3,2,1,0:T(8,128)(2,1)} %param.8, bf16[4,128,256]{2,1,0:T(8,128)(2,1)S(1)} %bitcast_select_fusion), kind=kOutput, calls=%fused_computation.260 | convolution fusion | flops 453083136 | bytes 5439488 | tf_op jit(solution)/shard_map/vtc,toc->vo/dot_general | solution.py:62
  43.7 2.6 %fusion.139 = bf16[1,128,256]{2,1,0:T(8,128)(2,1)S(1)} fusion(bf16[128,256]{1,0:T(8,128)(2,1)S(1)} %get-tuple-element.5, bf16[128,27,256]{2,0,1:T(8,128)(2,1)S(1)} %constant_dynamic-update-slice_fusion.189, bf16[1,2,27,256,256]{4,3,2,1,0:T(8,128)(2,1)} %param.8, bf16[4,128,256]{2,1,0:T(8,128)(2,1)S(1)} %bitcast_select_fusion), kind=kOutput, calls=%fused_computation.536 | convolution fusion | flops 453378048 | bytes 5505024 | tf_op jit(solution)/shard_map/vto,toi->vi/dot_general | solution.py:66
  46.4 0.8 maximum_bitcast_fusion
  47.3 84.0 %reduce-scatter.2.cloned.1.call-done = bf16[16,2,27,256]{3,0,2,1:T(8,128)(2,1)} async-done(((bf16[256,2,27,256]{3,0,2,1:T(8,128)(2,1)}), bf16[16,2,27,256]{3,0,2,1:T(8,128)(2,1)}) %reduce-scatter.2.cloned.1.call-update) | async-done | bytes 442384 | tf_op jit(solution)/shard_map/reduce_scatter | solution.py:93
  131.3 2.1 %fusion.102 = f32[1,2,27,16,256]{4,3,2,1,0:T(8,128)} fusion(bf16[16,2,27,256]{3,0,2,1:T(8,128)(2,1)} %reduce-scatter.2.cloned.1.call-done, f32[1,2,27,16,256]{4,3,2,1,0:T(8,128)S(1)} %copy-done), kind=kLoop, calls=%fused_computation.264 | loop fusion | flops 884736 | bytes 2211840 | tf_op jit(solution)/shard_map/broadcast_in_dim | solution.py:99
  (248 shorter events, 3.6 us)
Async XLA Ops:
  7.2 124.1 %reduce-scatter.2.cloned.1.call-start = ((), (), s32[]{:S(2)}) async-start(), calls=%async_computation.1 | async-start | bytes 7520256 | tf_op jit(solution)/shard_map/reduce_scatter | solution.py:93
  8.1 3.1 %copy-start.2 = (bf16[1,2,27,256,256]{4,3,2,1,0:T(8,128)(2,1)S(1)}, bf16[1,2,27,256,256]{4,3,2,1,0:T(8,128)(2,1)}, u32[]{:S(2)}) copy-start(bf16[1,2,27,256,256]{4,3,2,1,0:T(8,128)(2,1)} %param.8) | copy-start | bytes 21233668
  8.5 1.1 copy-start.1
  16.4 10.6 %collective-permute-start = (bf16[4,128,256]{2,1,0:T(8,128)(2,1)S(1)}, bf16[4,128,256]{2,1,0:T(8,128)(2,1)S(1)}, u32[]{:S(2)}, u32[]{:S(2)}) collective-permute-start(bf16[4,128,256]{2,1,0:T(8,128)(2,1)S(1)} %get-tuple-element.7), channel_id=1, source_target_pairs={{16,0},{17,1},{18,2},{19,3},{20,4},{21,5},{22,6},{23,7},{24,8},{25... | collective-permute-start | bytes 786440 | tf_op jit(solution)/shard_map/ppermute | solution.py:15
  22.5 6.5 %slice-start.2 = ((s8[7077888]{0:T(1024)(128)(4,1)}), s8[4194304]{0:T(1024)(128)(4,1)S(1)}, s32[]{:S(2)}) async-start(s8[7077888]{0:T(1024)(128)(4,1)} %bitcast.749), calls=%async_computation.4 | async-start | bytes 8388608
  28.0 1.8 %slice-start.3 = ((s8[7077888]{0:T(1024)(128)(4,1)}), s8[2883584]{0:T(1024)(128)(4,1)S(1)}, s32[]{:S(2)}) async-start(s8[7077888]{0:T(1024)(128)(4,1)} %bitcast.749), calls=%async_computation.5 | async-start | bytes 5767168
  32.1 2.2 %slice-start = ((s8[7077888]{0:T(1024)(128)(4,1)}), s8[4194304]{0:T(1024)(128)(4,1)S(1)}, s32[]{:S(2)}) async-start(s8[7077888]{0:T(1024)(128)(4,1)} %bitcast.521), calls=%async_computation.2 | async-start | bytes 8388608
  32.1 3.1 %slice-start.1 = ((s8[7077888]{0:T(1024)(128)(4,1)}), s8[2883584]{0:T(1024)(128)(4,1)S(1)}, s32[]{:S(2)}) async-start(s8[7077888]{0:T(1024)(128)(4,1)} %bitcast.521), calls=%async_computation.3 | async-start | bytes 5767168
  46.4 84.9 %copy-start = (f32[1,2,27,16,256]{4,3,2,1,0:T(8,128)S(1)}, f32[1,2,27,16,256]{4,3,2,1,0:T(8,128)}, u32[]{:S(2)}) copy-start(f32[1,2,27,16,256]{4,3,2,1,0:T(8,128)} %param.9) | copy-start | bytes 2654212
Sparse Core Ops, SparseCore 0:
  40.0 91.2 reduce-scatter.1
where the time goes:
time: 141 us; the launch traced here: 140 us
  waiting for transfers between devices  87.4 us (62%)
  matrix products  19.1 us (14%)
  between operations  16.7 us (12%)
  other arithmetic  8.65 us (6%)
  local copies, waits for them, and re-layouts  6.95 us (5%)
  starting transfers between devices  1.51 us (1%)
    reduce_scatter x1, waiting for transfers between devices, body(): lax.psum_scatter(both.astype(jnp.bfloat16), 'dp', scatter_dimension=0, ti...  84 us
    unnamed x215, local copies, waits for them, and re-layouts  5.8 us
    dot_general x2, matrix products, half_f(): jnp.einsum('vo,vti->oti', dx_one, patch_two, preferred_element_type=jnp.f...  5.12 us
    dot_general x2, matrix products, half_f(): jnp.einsum('vtc,toc->vo', patch_two, weight_f, preferred_element_type=jnp...  4.54 us
    another operation x1, other arithmetic, body(): jnp.stack([total_f, total_g], axis=1).astype(jnp.bfloat16)  3.49 us
    ppermute x1, waiting for transfers between devices, shifted(): return lax.ppermute(array, axis, pairs)  3.31 us
    dot_general x2, matrix products, half_f(): jnp.einsum('vto,toi->vi', back_one, weight_f, preferred_element_type=jnp....  3.29 us
  transfers between devices with their start and end apart: 2, of which 2 were waited for; matrix products, arithmetic and copies ran while one was open for 9% of the time, Pallas kernels for 0%

commit v1 on v0

v1 whole, which is shorter than its diff:
```python
import functools

import jax
import jax.numpy as jnp
from jax import lax
from jax.experimental import pallas as pl
from jax.experimental.pallas import tpu as pltpu
from jax.sharding import PartitionSpec as P

TD = 2
TH = 8
TW = 8
TICKS = 2
VOX = TD * TH * TW
PLANE = TH * TW
TAPS = 27
LANES = 128
MESH = pl.DeviceIdType.MESH


def tap_offset(tap):
    return tap // 9 - 1, (tap // 3) % 3 - 1, tap % 3 - 1


def sigmoid(u):
    return 1.0 / (1.0 + jnp.exp(-u))


def silu_grad(u, s):
    return s * (1.0 + u * (1.0 - s))


def fill(even, odd, x):
    row = lax.broadcasted_iota(jnp.int32, x.shape, 0)
    w = row % TW
    edge = jnp.zeros((TW, x.shape[1]), jnp.float32)
    for wi, dw in enumerate((-1, 0, 1)):
        s = x
        if dw:
            s = pltpu.roll(x, (-dw) % VOX, 0)
            s = jnp.where((w + dw >= 0) & (w + dw < TW), s, 0.0)
        for d in range(TD):
            plane = s[d * PLANE:(d + 1) * PLANE]
            odd[wi, d + 1] = plane.astype(jnp.bfloat16)
            even[wi, d + 1] = jnp.concatenate([edge, plane, edge], 0).astype(jnp.bfloat16)


def patch(even, odd, tap):
    dd, dh, dw = tap_offset(tap)
    if dh == 0:
        cut = odd[dw + 1, dd + 1:dd + 1 + TD]
    else:
        lo = (dh + 1) * TW
        cut = even[dw + 1, dd + 1:dd + 1 + TD, lo:lo + PLANE]
    return cut.reshape(VOX, cut.shape[-1])


def kernel(n, nsec, plan, incoming, feed, weights, up, grad,
           w_ref, nxt, ea, oa, eb, ob, a_send, d_send, a_recv, d_recv, big, acc, g_send, g_recv,
           w_sem, sec_s, sec_r, as_s, as_r, ds_s, ds_r, g_s, g_r):
    me = lax.axis_index("dp")
    sec = lax.axis_index("section")
    core = lax.rem(me, 2)
    chip = me // 2
    mate = me + 1 - 2 * core
    block = d_recv.shape[2]
    half = block // 2
    last = sec == nsec - 1
    loads = [pltpu.make_async_copy(weights.at[0, b], w_ref.at[b], w_sem.at[b]) for b in (0, 1)]
    loads[1].start()
    loads[0].start()

    barrier = pltpu.get_barrier_semaphore()

    @pl.loop(1, n)
    def _(k):
        pl.semaphore_signal(barrier, inc=1, device_id={"dp": lax.rem(me + k, n)}, device_id_type=MESH)

    @pl.when(sec > 0)
    def _():
        pl.semaphore_signal(barrier, inc=1, device_id={"section": sec - 1}, device_id_type=MESH)

    @pl.when(sec < nsec - 1)
    def _():
        pl.semaphore_signal(barrier, inc=1, device_id={"section": sec + 1}, device_id_type=MESH)

    for wi in range(3):
        for ref in (ea, oa, eb, ob):
            for d in (0, TD + 1):
                ref[wi, d] = jnp.zeros(ref.shape[2:], jnp.bfloat16)

    @pl.when(last)
    def _():
        nxt[...] = feed[plan[0, 0]]

    extra = jnp.where(sec > 0, 1, 0) + jnp.where(sec < nsec - 1, 1, 0)
    pl.semaphore_wait(barrier, n - 1 + extra)

    def a_copy(stage, peer, slot):
        return pltpu.make_async_remote_copy(
            src_ref=a_send.at[stage, lax.rem(peer, 2)], dst_ref=a_recv.at[stage, slot],
            send_sem=as_s.at[stage, peer], recv_sem=as_r.at[stage, slot],
            device_id={"dp": peer}, device_id_type=MESH)

    def d_copy(stage, peer, slot):
        return pltpu.make_async_remote_copy(
            src_ref=d_send.at[stage, peer // 2], dst_ref=d_recv.at[stage, slot],
            send_sem=ds_s.at[stage, peer], recv_sem=ds_r.at[stage, slot],
            device_id={"dp": peer}, device_id_type=MESH)

    def share(stage, act, err):
        a_send[stage, 0] = act[:, :LANES]
        a_send[stage, 1] = act[:, LANES:]
        turned = jnp.transpose(err).astype(jnp.bfloat16)
        d_send[stage] = turned.reshape(d_send.shape[1:])
        a_recv[stage, me] = a_send[stage, core]
        d_recv[stage, me] = d_send[stage, chip]

        @pl.loop(1, n)
        def _(k):
            peer = lax.rem(me + k, n)
            d_copy(stage, peer, me).start()
            a_copy(stage, peer, me).start()

    def convs(b):
        fwd = jnp.zeros((VOX, w_ref.shape[2]), jnp.float32)
        for tap in range(TAPS):
            fwd += lax.dot_general(patch(ea, oa, tap), w_ref[b, tap], (((1,), (1,)), ((), ())),
                                   preferred_element_type=jnp.float32)
        bwd = jnp.zeros((VOX, w_ref.shape[3]), jnp.float32)
        for tap in range(TAPS):
            bwd += jnp.dot(patch(eb, ob, TAPS - 1 - tap), w_ref[b, tap],
                           preferred_element_type=jnp.float32)
        return fwd, bwd

    def sec_copy(j):
        return pltpu.make_async_remote_copy(
            src_ref=up.at[0, j], dst_ref=nxt.at[j], send_sem=sec_s.at[j], recv_sem=sec_r.at[j],
            device_id={"section": lax.rem(sec + nsec - 1, nsec)}, device_id_type=MESH)

    for tick in range(TICKS):
        if tick == 0:
            cur = incoming.at[0]
        else:
            cur = nxt

            @pl.when(sec < nsec - 1)
            def _():
                for j in range(4):
                    sec_copy(j).wait_recv()
        y1 = cur[0].astype(jnp.float32)
        s1 = sigmoid(y1)
        a1 = y1 * s1
        dy2 = cur[3].astype(jnp.float32)
        share(2 * tick, a1.astype(jnp.bfloat16), dy2)
        fill(ea, oa, a1)
        fill(eb, ob, dy2)
        if tick == 0:
            loads[1].wait()
        fwd, bwd = convs(1)
        x2 = (cur[1].astype(jnp.float32) - fwd).astype(jnp.bfloat16)
        dx1 = (cur[2].astype(jnp.float32) + bwd * silu_grad(y1, s1)).astype(jnp.bfloat16)
        up[tick, 1] = x2
        up[tick, 2] = dx1
        if tick == 0:
            @pl.when(sec > 0)
            def _():
                sec_copy(1).start()
                sec_copy(2).start()
        u = x2.astype(jnp.float32)
        s2 = sigmoid(u)
        a2 = u * s2
        e1 = dx1.astype(jnp.float32)
        share(2 * tick + 1, a2.astype(jnp.bfloat16), e1)
        fill(ea, oa, a2)
        fill(eb, ob, e1)
        if tick == 0:
            loads[0].wait()
        fwd, bwd = convs(0)
        u = up[tick, 1].astype(jnp.float32)
        s2 = sigmoid(u)
        up[tick, 0] = (cur[0].astype(jnp.float32) - fwd).astype(jnp.bfloat16)
        up[tick, 3] = (cur[3].astype(jnp.float32) + bwd * silu_grad(u, s2)).astype(jnp.bfloat16)
        if tick == 0:
            @pl.when(sec > 0)
            def _():
                sec_copy(0).start()
                sec_copy(3).start()

    lane = lax.broadcasted_iota(jnp.int32, (block, VOX), 1)
    ld, lh, lw = lane // PLANE, (lane // TW) % TH, lane % TW

    def g_copy(b):
        return pltpu.make_async_remote_copy(
            src_ref=g_send.at[b], dst_ref=g_recv.at[b], send_sem=g_s.at[b], recv_sem=g_r.at[b],
            device_id={"dp": mate}, device_id_type=MESH)

    tiles = 3
    per = TAPS * block // tiles
    for stage in range(2 * TICKS):
        b = stage % 2

        @pl.loop(1, n)
        def _(k):
            peer = lax.rem(me + k, n)
            d_copy(stage, me, peer).wait_recv()
            a_copy(stage, me, peer).wait_recv()

        @pl.loop(0, n)
        def _(r):
            x = d_recv[stage, r].astype(jnp.float32)
            cols = pl.ds(pl.multiple_of(r * VOX, VOX), VOX)
            for tap in range(TAPS):
                dd, dh, dw = tap_offset(tap)
                flat = dd * PLANE + dh * TW + dw
                s = x if flat == 0 else pltpu.roll(x, flat % VOX, 1)
                ok = None
                for c, by, size in ((ld, dd, TD), (lh, dh, TH), (lw, dw, TW)):
                    if by:
                        this = c >= 1 if by > 0 else c < size - 1
                        ok = this if ok is None else ok & this
                if ok is not None:
                    s = jnp.where(ok, s, 0.0)
                big[tap * block:(tap + 1) * block, cols] = s.astype(jnp.bfloat16)

        @pl.loop(0, tiles)
        def _(m):
            rows = pl.ds(pl.multiple_of(m * per, 16), per)
            got = jnp.dot(big[rows, :], a_recv[stage].reshape(n * VOX, LANES),
                          preferred_element_type=jnp.float32)
            if stage < 2:
                acc[b, rows, :] = got
            else:
                acc[b, rows, :] += got
        if stage >= 2 * TICKS - 2:
            view = acc.at[b]
            for tap in range(TAPS):
                lo = pl.multiple_of(tap * block + (1 - core) * half, 8)
                g_send[b, tap] = view[pl.ds(lo, half), :]
            g_copy(b).start()
    mine = pl.ds(pl.multiple_of(core * LANES, LANES), LANES)
    other = pl.ds(pl.multiple_of((1 - core) * LANES, LANES), LANES)
    for b in (0, 1):
        for tap in range(TAPS):
            lo = pl.multiple_of(tap * block + core * half, 8)
            grad[1 - b, tap, :, mine] = acc[b, pl.ds(lo, half), :]
    for b in (0, 1):
        g_copy(b).wait_recv()
        grad[1 - b, :, :, other] = g_recv[b]
    for b in (0, 1):
        g_copy(b).wait_send()
    for stage in range(2 * TICKS):
        @pl.loop(1, n)
        def _(k):
            peer = lax.rem(me + k, n)
            d_copy(stage, peer, me).wait_send()
            a_copy(stage, peer, me).wait_send()

    @pl.when(sec > 0)
    def _():
        for j in range(4):
            sec_copy(j).wait_send()


def body(incoming, feed, plan, weights, momentum):
    n = lax.axis_size("dp")
    nsec = lax.axis_size("section")
    channels = weights.shape[-1]
    block = 2 * channels // n
    stages = 2 * TICKS
    bf, f32 = jnp.bfloat16, jnp.float32
    vm = pl.BlockSpec(memory_space=pltpu.VMEM)
    dma = pltpu.SemaphoreType.DMA
    up, grad = pl.pallas_call(
        functools.partial(kernel, n, nsec),
        out_shape=(
            jax.ShapeDtypeStruct((TICKS, 4, VOX, channels), bf),
            jax.ShapeDtypeStruct((2, TAPS, block // 2, channels), f32),
        ),
        in_specs=[pl.BlockSpec(memory_space=pltpu.SMEM), vm, vm, pl.BlockSpec(memory_space=pl.ANY)],
        out_specs=(vm, vm),
        scratch_shapes=[
            pltpu.VMEM(weights.shape[1:], bf),
            pltpu.VMEM((4, VOX, channels), bf),
            pltpu.VMEM((3, TD + 2, PLANE + 2 * TW, channels), bf),
            pltpu.VMEM((3, TD + 2, PLANE, channels), bf),
            pltpu.VMEM((3, TD + 2, PLANE + 2 * TW, channels), bf),
            pltpu.VMEM((3, TD + 2, PLANE, channels), bf),
            pltpu.VMEM((stages, 2, VOX, LANES), bf),
            pltpu.VMEM((stages, n // 2, block, VOX), bf),
            pltpu.VMEM((stages, n, VOX, LANES), bf),
            pltpu.VMEM((stages, n, block, VOX), bf),
            pltpu.VMEM((TAPS * block, n * VOX), bf),
            pltpu.VMEM((2, TAPS * block, LANES), f32),
            pltpu.VMEM((2, TAPS, block // 2, LANES), f32),
            pltpu.VMEM((2, TAPS, block // 2, LANES), f32),
            dma((2,)), dma((4,)), dma((4,)),
            dma((stages, n)), dma((stages, n)), dma((stages, n)), dma((stages, n)),
            dma((2,)), dma((2,)),
        ],
        compiler_params=pltpu.CompilerParams(
            collective_id=0, has_side_effects=True, vmem_limit_bytes=48 * 1024 * 1024),
        cost_estimate=pl.CostEstimate(flops=12 * TICKS * VOX * TAPS * channels * channels,
                                      bytes_accessed=weights.size * 2, transcendentals=0),
    )(plan, incoming, feed, weights)
    new_momentum = 0.9 * momentum[0] + grad / (n * TICKS)
    return (up[:, None], new_momentum[None])


def solution(mesh):
    in_specs = (
        P("section", None, "dp", None),
        P(None, None, "dp", None),
        P(None, "dp"),
        P("section", None, None, None, None),
        P("section", None, None, "dp", None),
    )
    out_specs = (P(None, "section", None, "dp", None), P("section", None, None, "dp", None))
    return jax.shard_map(body, mesh=mesh, in_specs=in_specs, out_specs=out_specs, check_vma=False)
```

time: 141 us -> 75.1 us (0.53)
  the two profiles are of different devices: /device:TPU:0 before, /device:TPU:15 now
where the time goes in v1:
time: 75.1 us; the launch traced here: 74.9 us
  Pallas kernels  69.6 us (93%)
  local copies, waits for them, and re-layouts  2.96 us (4%)
  between operations  1.3 us (2%)
  other arithmetic  1.1 us (1%)
    pallas_call x1, Pallas kernels, body(): pl.pallas_call(functools.partial(kernel, n, nsec), out_shape=(jax.ShapeDt...  69.6 us
    unnamed x7, local copies, waits for them, and re-layouts  2.96 us

profile of v1, /device:TPU:15, one launch (start us, length us, event | category | flops | bytes accessed | tf_op | source)
XLA Modules:
  0.0 74.9 jit_solution(9075467804189313245)
XLA Ops:
  1.3 0.0 copy-start
  1.3 1.2 %copy-done = bf16[4,4,128,256]{3,2,1,0:T(8,128)(2,1)S(1)} copy-done((bf16[4,4,128,256]{3,2,1,0:T(8,128)(2,1)S(1)}, bf16[4,4,128,256]{3,2,1,0:T(8,128)(2,1)}, u32[]{:S(2)}) %copy-start) | copy-done | bytes 1048600
  2.5 0.0 copy-start.1
  2.5 0.9 %copy-done.1 = bf16[1,4,128,256]{3,2,1,0:T(8,128)(2,1)S(1)} copy-done((bf16[1,4,128,256]{3,2,1,0:T(8,128)(2,1)S(1)}, bf16[1,4,128,256]{3,2,1,0:T(8,128)(2,1)}, u32[]{:S(2)}) %copy-start.1) | copy-done | bytes 262168
  3.5 0.0 copy-start.2
  3.5 69.6 %shard_map.68 = (bf16[2,4,128,256]{3,2,1,0:T(8,128)(2,1)S(1)}, f32[2,27,16,256]{3,2,1,0:T(8,128)S(1)}) custom-call(s32[1,1]{1,0:T(1,128)S(6)} %copy.9.plan, bf16[1,4,128,256]{3,2,1,0:T(8,128)(2,1)S(1)} %copy-done.1, bf16[4,4,128,256]{3,2,1,0:T(8,128)(2,1)S(1)} %copy-done, bf16[1,2,27,256,256]{4,3,2,1,0:T(8,128)(2,1)} %weights.1), custom_call_target="tpu_custom_call" | custom-call | flops 5435817984 | bytes 7077888 | tf_op jit(solution)/shard_map/pallas_call | solution.py:274
  73.0 0.0 copy-done.2
  73.0 1.1 %fusion = f32[1,2,27,16,256]{4,3,2,1,0:T(8,128)} fusion(f32[2,27,16,256]{3,2,1,0:T(8,128)S(1)} %get-tuple-element.5, f32[1,2,27,16,256]{4,3,2,1,0:T(8,128)S(1)} %copy-done.2), kind=kLoop, calls=%fused_computation.1 | loop fusion | flops 663552 | bytes 2654208 | tf_op jit(solution)/shard_map/broadcast_in_dim | solution.py:307
  74.2 0.8 %copy.10 = bf16[2,1,4,128,256]{4,3,2,1,0:T(8,128)(2,1)} copy(bf16[2,1,4,128,256]{4,3,2,1,0:T(8,128)(2,1)S(1)} %bitcast.9) | data formatting | bytes 1048576
Async XLA Ops:
  1.3 1.2 %copy-start = (bf16[4,4,128,256]{3,2,1,0:T(8,128)(2,1)S(1)}, bf16[4,4,128,256]{3,2,1,0:T(8,128)(2,1)}, u32[]{:S(2)}) copy-start(bf16[4,4,128,256]{3,2,1,0:T(8,128)(2,1)} %feed.1) | copy-start | bytes 3145732
  2.5 0.9 %copy-start.1 = (bf16[1,4,128,256]{3,2,1,0:T(8,128)(2,1)S(1)}, bf16[1,4,128,256]{3,2,1,0:T(8,128)(2,1)}, u32[]{:S(2)}) copy-start(bf16[1,4,128,256]{3,2,1,0:T(8,128)(2,1)} %incoming.1) | copy-start | bytes 786436
  3.5 69.6 %copy-start.2 = (f32[1,2,27,16,256]{4,3,2,1,0:T(8,128)S(1)}, f32[1,2,27,16,256]{4,3,2,1,0:T(8,128)}, u32[]{:S(2)}) copy-start(f32[1,2,27,16,256]{4,3,2,1,0:T(8,128)} %param.9) | copy-start | bytes 2654212

commit v2 on v1

--- a/solution.py
+++ b/solution.py
@@ -56,25 +56,43 @@
 
 
 def kernel(n, nsec, plan, incoming, feed, weights, up, grad,
-           w_ref, nxt, ea, oa, eb, ob, a_send, d_send, a_recv, d_recv, big, acc, g_send, g_recv,
-           w_sem, sec_s, sec_r, as_s, as_r, ds_s, ds_r, g_s, g_r):
+           w_ref, first, pool, nxt, upv, ea, oa, eb, ob, a_send, d_send, d_mid, a_recv, d_recv, big, acc,
+           g_send, g_recv, w_sem, in_sem, up_sem, sec_s, sec_r, as_s, as_r, ar_s, ar_r,
+           dz_s, dz_r, dy_s, dy_r, dm_s, dm_r, g_s, g_r):
     me = lax.axis_index("dp")
     sec = lax.axis_index("section")
+    ny, nz = a_recv.shape[1:3]
     core = lax.rem(me, 2)
-    chip = me // 2
+    y = lax.rem(me // 2, ny)
+    z = me // (2 * ny)
     mate = me + 1 - 2 * core
-    block = d_recv.shape[2]
+    block = d_recv.shape[-2]
     half = block // 2
     last = sec == nsec - 1
+
+    def at(zz, yy, cc):
+        return (zz * ny + yy) * 2 + cc
+
+    def z_of(k):
+        return lax.rem(z + k, nz)
+
+    def y_of(k):
+        return lax.rem(y + k, ny)
+
+    load_in = pltpu.make_async_copy(incoming.at[0], first, in_sem.at[0])
+    load_pool = pltpu.make_async_copy(feed, pool, in_sem.at[1])
     loads = [pltpu.make_async_copy(weights.at[0, b], w_ref.at[b], w_sem.at[b]) for b in (0, 1)]
+    load_in.start()
     loads[1].start()
     loads[0].start()
+    load_pool.start()
 
     barrier = pltpu.get_barrier_semaphore()
-
-    @pl.loop(1, n)
-    def _(k):
-        pl.semaphore_signal(barrier, inc=1, device_id={"dp": lax.rem(me + k, n)}, device_id_type=MESH)
+    peers = [mate]
+    peers += [at(z_of(k), y, cc) for k in range(1, nz) for cc in (0, 1)]
+    peers += [at(z, y_of(k), cc) for k in range(1, ny) for cc in (0, 1)]
+    for peer in peers:
+        pl.semaphore_signal(barrier, inc=1, device_id={"dp": peer}, device_id_type=MESH)
 
     @pl.when(sec > 0)
     def _():
@@ -88,45 +106,107 @@
         for ref in (ea, oa, eb, ob):
             for d in (0, TD + 1):
                 ref[wi, d] = jnp.zeros(ref.shape[2:], jnp.bfloat16)
-
-    @pl.when(last)
-    def _():
-        nxt[...] = feed[plan[0, 0]]
-
+    load_in.wait()
     extra = jnp.where(sec > 0, 1, 0) + jnp.where(sec < nsec - 1, 1, 0)
-    pl.semaphore_wait(barrier, n - 1 + extra)
-
-    def a_copy(stage, peer, slot):
-        return pltpu.make_async_remote_copy(
-            src_ref=a_send.at[stage, lax.rem(peer, 2)], dst_ref=a_recv.at[stage, slot],
-            send_sem=as_s.at[stage, peer], recv_sem=as_r.at[stage, slot],
+    pl.semaphore_wait(barrier, len(peers) + extra)
+
+    def a_direct(stage, idx, peer, to, slot):
+        return pltpu.make_async_remote_copy(
+            src_ref=a_send.at[stage, to], dst_ref=a_recv.at[(stage,) + slot],
+            send_sem=as_s.at[stage, idx], recv_sem=as_r.at[(stage,) + slot],
             device_id={"dp": peer}, device_id_type=MESH)
 
-    def d_copy(stage, peer, slot):
-        return pltpu.make_async_remote_copy(
-            src_ref=d_send.at[stage, peer // 2], dst_ref=d_recv.at[stage, slot],
-            send_sem=ds_s.at[stage, peer], recv_sem=ds_r.at[stage, slot],
-            device_id={"dp": peer}, device_id_type=MESH)
+    def a_relay(stage, yy, slot):
+        return pltpu.make_async_remote_copy(
+            src_ref=a_recv.at[(stage,) + slot], dst_ref=a_recv.at[(stage,) + slot],
+            send_sem=ar_s.at[stage, yy, slot[1]], recv_sem=ar_r.at[(stage,) + slot],
+            device_id={"dp": at(z, yy, core)}, device_id_type=MESH)
+
+    def d_along_z(stage, zz, slot):
+        return pltpu.make_async_remote_copy(
+            src_ref=d_send.at[stage, zz], dst_ref=d_mid.at[stage, :, slot],
+            send_sem=dz_s.at[stage, zz], recv_sem=dz_r.at[stage, slot],
+            device_id={"dp": at(zz, y, core)}, device_id_type=MESH)
+
+    def d_along_y(stage, yy, slot):
+        return pltpu.make_async_remote_copy(
+            src_ref=d_mid.at[stage, yy], dst_ref=d_recv.at[stage, core, slot],
+            send_sem=dy_s.at[stage, yy], recv_sem=dy_r.at[stage, slot],
+            device_id={"dp": at(z, yy, core)}, device_id_type=MESH)
+
+    def d_to_mate(stage, whose):
+        return pltpu.make_async_remote_copy(
+            src_ref=d_recv.at[stage, whose], dst_ref=d_recv.at[stage, whose],
+            send_sem=dm_s.at[stage], recv_sem=dm_r.at[stage],
+            device_id={"dp": mate}, device_id_type=MESH)
+
+    def directs(stage):
+        mine = (y, z, core)
+        out = []
+        for k in range(1, nz):
+            for cc in (0, 1):
+                out.append(a_direct(stage, len(out), at(z_of(k), y, cc), cc, mine))
+        for k in range(1, ny):
+            for cc in (0, 1):
+                out.append(a_direct(stage, len(out), at(z, y_of(k), cc), cc, mine))
+        out.append(a_direct(stage, len(out), mate, 1 - core, mine))
+        return out
 
     def share(stage, act, err):
         a_send[stage, 0] = act[:, :LANES]
         a_send[stage, 1] = act[:, LANES:]
         turned = jnp.transpose(err).astype(jnp.bfloat16)
         d_send[stage] = turned.reshape(d_send.shape[1:])
-        a_recv[stage, me] = a_send[stage, core]
-        d_recv[stage, me] = d_send[stage, chip]
-
-        @pl.loop(1, n)
-        def _(k):
-            peer = lax.rem(me + k, n)
-            d_copy(stage, peer, me).start()
-            a_copy(stage, peer, me).start()
-
-    def convs(b):
+        for k in range(1, nz):
+            d_along_z(stage, z_of(k), z).start()
+        for copy in directs(stage):
+            copy.start()
+        a_recv[stage, y, z, core] = a_send[stage, core]
+        for yy in range(ny):
+            d_mid[stage, yy, z] = d_send[stage, z, yy]
+
+    def relay(stage):
+        for k in range(1, nz):
+            d_along_z(stage, z, z_of(k)).wait_recv()
+        for k in range(1, ny):
+            d_along_y(stage, y_of(k), y).start()
+        d_recv[stage, core, y] = d_mid[stage, y]
+        for k in range(1, nz):
+            for cc in (0, 1):
+                a_direct(stage, 0, mate, 0, (y, z_of(k), cc)).wait_recv()
+            for j in range(1, ny):
+                a_relay(stage, y_of(j), (y, z_of(k))).start()
+
+    def swap_errors(stage):
+        for k in range(1, ny):
+            d_along_y(stage, y, y_of(k)).wait_recv()
+        d_to_mate(stage, core).start()
+
+    def arrive(stage):
+        a_direct(stage, 0, mate, 0, (y, z, 1 - core)).wait_recv()
+        for j in range(1, ny):
+            for cc in (0, 1):
+                a_direct(stage, 0, mate, 0, (y_of(j), z, cc)).wait_recv()
+            for k in range(1, nz):
+                a_relay(stage, y, (y_of(j), z_of(k))).wait_recv()
+
+    def sent(stage):
+        for k in range(1, nz):
+            d_along_z(stage, z_of(k), z).wait_send()
+        for copy in directs(stage):
+            copy.wait_send()
+        for j in range(1, ny):
+            d_along_y(stage, y_of(j), y).wait_send()
+            for k in range(1, nz):
+                a_relay(stage, y_of(j), (y, z_of(k))).wait_send()
+        d_to_mate(stage, core).wait_send()
+
+    def convs(b, hook):
         fwd = jnp.zeros((VOX, w_ref.shape[2]), jnp.float32)
         for tap in range(TAPS):
             fwd += lax.dot_general(patch(ea, oa, tap), w_ref[b, tap], (((1,), (1,)), ((), ())),
                                    preferred_element_type=jnp.float32)
+        hook()
         bwd = jnp.zeros((VOX, w_ref.shape[3]), jnp.float32)
         for tap in range(TAPS):
             bwd += jnp.dot(patch(eb, ob, TAPS - 1 - tap), w_ref[b, tap],
@@ -135,14 +215,19 @@
 
     def sec_copy(j):
         return pltpu.make_async_remote_copy(
-            src_ref=up.at[0, j], dst_ref=nxt.at[j], send_sem=sec_s.at[j], recv_sem=sec_r.at[j],
+            src_ref=upv.at[0, j], dst_ref=nxt.at[j], send_sem=sec_s.at[j], recv_sem=sec_r.at[j],
             device_id={"section": lax.rem(sec + nsec - 1, nsec)}, device_id_type=MESH)
 
     for tick in range(TICKS):
         if tick == 0:
-            cur = incoming.at[0]
+            cur = first
         else:
             cur = nxt
+            load_pool.wait()
+
+            @pl.when(last)
+            def _():
+                nxt[...] = pool[plan[0, 0]]
 
             @pl.when(sec < nsec - 1)
             def _():
@@ -157,11 +242,11 @@
         fill(eb, ob, dy2)
         if tick == 0:
             loads[1].wait()
-        fwd, bwd = convs(1)
+        fwd, bwd = convs(1, lambda: relay(2 * tick - 1) if tick else None)
         x2 = (cur[1].astype(jnp.float32) - fwd).astype(jnp.bfloat16)
         dx1 = (cur[2].astype(jnp.float32) + bwd * silu_grad(y1, s1)).astype(jnp.bfloat16)
-        up[tick, 1] = x2
-        up[tick, 2] = dx1
+        upv[tick, 1] = x2
+        upv[tick, 2] = dx1
         if tick == 0:
             @pl.when(sec > 0)
             def _():
@@ -176,16 +261,17 @@
         fill(eb, ob, e1)
         if tick == 0:
             loads[0].wait()
-        fwd, bwd = convs(0)
-        u = up[tick, 1].astype(jnp.float32)
+        fwd, bwd = convs(0, lambda: relay(2 * tick))
+        u = upv[tick, 1].astype(jnp.float32)
         s2 = sigmoid(u)
-        up[tick, 0] = (cur[0].astype(jnp.float32) - fwd).astype(jnp.bfloat16)
-        up[tick, 3] = (cur[3].astype(jnp.float32) + bwd * silu_grad(u, s2)).astype(jnp.bfloat16)
+        upv[tick, 0] = (cur[0].astype(jnp.float32) - fwd).astype(jnp.bfloat16)
+        upv[tick, 3] = (cur[3].astype(jnp.float32) + bwd * silu_grad(u, s2)).astype(jnp.bfloat16)
         if tick == 0:
             @pl.when(sec > 0)
             def _():
                 sec_copy(0).start()
                 sec_copy(3).start()
+        pltpu.make_async_copy(upv.at[tick], up.at[tick], up_sem.at[tick]).start()
 
     lane = lax.broadcasted_iota(jnp.int32, (block, VOX), 1)
     ld, lh, lw = lane // PLANE, (lane // TW) % TH, lane % TW
@@ -197,18 +283,19 @@
 
     tiles = 3
     per = TAPS * block // tiles
-    for stage in range(2 * TICKS):
+    stages = 2 * TICKS
+    relay(stages - 1)
+    swap_errors(0)
+    for stage in range(stages):
         b = stage % 2
-
-        @pl.loop(1, n)
-        def _(k):
-            peer = lax.rem(me + k, n)
-            d_copy(stage, me, peer).wait_recv()
-            a_copy(stage, me, peer).wait_recv()
+        if stage + 1 < stages:
+            swap_errors(stage + 1)
+        d_to_mate(stage, 1 - core).wait_recv()
+        arrive(stage)
 
         @pl.loop(0, n)
         def _(r):
-            x = d_recv[stage, r].astype(jnp.float32)
+            x = d_recv[stage, lax.rem(r, 2), r // (2 * nz), lax.rem(r // 2, nz)].astype(jnp.float32)
             cols = pl.ds(pl.multiple_of(r * VOX, VOX), VOX)
             for tap in range(TAPS):
                 dd, dh, dw = tap_offset(tap)
@@ -249,12 +336,10 @@
         grad[1 - b, :, :, other] = g_recv[b]
     for b in (0, 1):
         g_copy(b).wait_send()
-    for stage in range(2 * TICKS):
-        @pl.loop(1, n)
-        def _(k):
-            peer = lax.rem(me + k, n)
-            d_copy(stage, peer, me).wait_send()
-            a_copy(stage, peer, me).wait_send()
+    for stage in range(stages):
+        sent(stage)
+    for tick in range(TICKS):
+        pltpu.make_async_copy(upv.at[tick], up.at[tick], up_sem.at[tick]).wait()
 
     @pl.when(sec > 0)
     def _():
@@ -267,9 +352,12 @@
     nsec = lax.axis_size("section")
     channels = weights.shape[-1]
     block = 2 * channels // n
+    ny = max(1, n // 8)
+    nz = n // (2 * ny)
     stages = 2 * TICKS
     bf, f32 = jnp.bfloat16, jnp.float32
     vm = pl.BlockSpec(memory_space=pltpu.VMEM)
+    hbm = pl.BlockSpec(memory_space=pl.ANY)
     dma = pltpu.SemaphoreType.DMA
     up, grad = pl.pallas_call(
         functools.partial(kernel, n, nsec),
@@ -277,26 +365,31 @@
             jax.ShapeDtypeStruct((TICKS, 4, VOX, channels), bf),
             jax.ShapeDtypeStruct((2, TAPS, block // 2, channels), f32),
         ),
-        in_specs=[pl.BlockSpec(memory_space=pltpu.SMEM), vm, vm, pl.BlockSpec(memory_space=pl.ANY)],
-        out_specs=(vm, vm),
+        in_specs=[pl.BlockSpec(memory_space=pltpu.SMEM), hbm, hbm, hbm],
+        out_specs=(hbm, vm),
         scratch_shapes=[
             pltpu.VMEM(weights.shape[1:], bf),
             pltpu.VMEM((4, VOX, channels), bf),
+            pltpu.VMEM(feed.shape, bf),
+            pltpu.VMEM((4, VOX, channels), bf),
+            pltpu.VMEM((TICKS, 4, VOX, channels), bf),
             pltpu.VMEM((3, TD + 2, PLANE + 2 * TW, channels), bf),
             pltpu.VMEM((3, TD + 2, PLANE, channels), bf),
             pltpu.VMEM((3, TD + 2, PLANE + 2 * TW, channels), bf),
             pltpu.VMEM((3, TD + 2, PLANE, channels), bf),
             pltpu.VMEM((stages, 2, VOX, LANES), bf),
-            pltpu.VMEM((stages, n // 2, block, VOX), bf),
-            pltpu.VMEM((stages, n, VOX, LANES), bf),
-            pltpu.VMEM((stages, n, block, VOX), bf),
+            pltpu.VMEM((stages, nz, ny, block, VOX), bf),
+            pltpu.VMEM((stages, ny, nz, block, VOX), bf),
+            pltpu.VMEM((stages, ny, nz, 2, VOX, LANES), bf),
+            pltpu.VMEM((stages, 2, ny, nz, block, VOX), bf),
             pltpu.VMEM((TAPS * block, n * VOX), bf),
             pltpu.VMEM((2, TAPS * block, LANES), f32),
             pltpu.VMEM((2, TAPS, block // 2, LANES), f32),
             pltpu.VMEM((2, TAPS, block // 2, LANES), f32),
-            dma((2,)), dma((4,)), dma((4,)),
-            dma((stages, n)), dma((stages, n)), dma((stages, n)), dma((stages, n)),
-            dma((2,)), dma((2,)),
+            dma((2,)), dma((2,)), dma((TICKS,)), dma((4,)), dma((4,)),
+            dma((stages, 2 * (ny + nz))), dma((stages, ny, nz, 2)), dma((stages, ny, nz)), dma((stages, ny, nz)),
+            dma((stages, nz)), dma((stages, nz)), dma((stages, ny)), dma((stages, ny)),
+            dma((stages,)), dma((stages,)), dma((2,)), dma((2,)),
         ],
         compiler_params=pltpu.CompilerParams(
             collective_id=0, has_side_effects=True, vmem_limit_bytes=48 * 1024 * 1024),

time: 75.1 us -> 59.6 us (0.79)
  the two profiles are of different devices: /device:TPU:15 before, /device:TPU:25 now
where the time goes in v2:
time: 59.6 us; the launch traced here: 59.4 us
  Pallas kernels  54.1 us (91%)
  local copies, waits for them, and re-layouts  2.96 us (5%)
  between operations  1.3 us (2%)
  other arithmetic  1.1 us (2%)
    pallas_call x1, Pallas kernels, body(): pl.pallas_call(functools.partial(kernel, n, nsec), out_shape=(jax.ShapeDt...  54.1 us
    unnamed x7, local copies, waits for them, and re-layouts  2.96 us

profile of v2, /device:TPU:25, one launch (start us, length us, event | category | flops | bytes accessed | tf_op | source)
XLA Modules:
  0.0 59.4 jit_solution(9417568538708871662)
XLA Ops:
  1.3 0.0 copy-start
  1.3 1.2 %copy-done = bf16[4,4,128,256]{3,2,1,0:T(8,128)(2,1)S(1)} copy-done((bf16[4,4,128,256]{3,2,1,0:T(8,128)(2,1)S(1)}, bf16[4,4,128,256]{3,2,1,0:T(8,128)(2,1)}, u32[]{:S(2)}) %copy-start) | copy-done | bytes 1048600
  2.5 0.0 copy-start.1
  2.5 0.9 %copy-done.1 = bf16[1,4,128,256]{3,2,1,0:T(8,128)(2,1)S(1)} copy-done((bf16[1,4,128,256]{3,2,1,0:T(8,128)(2,1)S(1)}, bf16[1,4,128,256]{3,2,1,0:T(8,128)(2,1)}, u32[]{:S(2)}) %copy-start.1) | copy-done | bytes 262168
  3.5 0.0 copy-start.2
  3.5 54.1 %shard_map.68 = (bf16[2,4,128,256]{3,2,1,0:T(8,128)(2,1)S(1)}, f32[2,27,16,256]{3,2,1,0:T(8,128)S(1)}) custom-call(s32[1,1]{1,0:T(1,128)S(6)} %copy.9.plan, bf16[1,4,128,256]{3,2,1,0:T(8,128)(2,1)S(1)} %copy-done.1, bf16[4,4,128,256]{3,2,1,0:T(8,128)(2,1)S(1)} %copy-done, bf16[1,2,27,256,256]{4,3,2,1,0:T(8,128)(2,1)} %weights.1), custom_call_target="tpu_custom_call" | custom-call | flops 5435817984 | bytes 7077888 | tf_op jit(solution)/shard_map/pallas_call | solution.py:362
  57.5 0.0 copy-done.2
  57.5 1.1 %fusion = f32[1,2,27,16,256]{4,3,2,1,0:T(8,128)} fusion(f32[2,27,16,256]{3,2,1,0:T(8,128)S(1)} %get-tuple-element.5, f32[1,2,27,16,256]{4,3,2,1,0:T(8,128)S(1)} %copy-done.2), kind=kLoop, calls=%fused_computation.1 | loop fusion | flops 663552 | bytes 2654208 | tf_op jit(solution)/shard_map/broadcast_in_dim | solution.py:400
  58.6 0.8 %copy.10 = bf16[2,1,4,128,256]{4,3,2,1,0:T(8,128)(2,1)} copy(bf16[2,1,4,128,256]{4,3,2,1,0:T(8,128)(2,1)S(1)} %bitcast.9) | data formatting | bytes 1048576
Async XLA Ops:
  1.3 1.2 %copy-start = (bf16[4,4,128,256]{3,2,1,0:T(8,128)(2,1)S(1)}, bf16[4,4,128,256]{3,2,1,0:T(8,128)(2,1)}, u32[]{:S(2)}) copy-start(bf16[4,4,128,256]{3,2,1,0:T(8,128)(2,1)} %feed.1) | copy-start | bytes 3145732
  2.5 0.9 %copy-start.1 = (bf16[1,4,128,256]{3,2,1,0:T(8,128)(2,1)S(1)}, bf16[1,4,128,256]{3,2,1,0:T(8,128)(2,1)}, u32[]{:S(2)}) copy-start(bf16[1,4,128,256]{3,2,1,0:T(8,128)(2,1)} %incoming.1) | copy-start | bytes 786436
  3.5 54.1 %copy-start.2 = (f32[1,2,27,16,256]{4,3,2,1,0:T(8,128)S(1)}, f32[1,2,27,16,256]{4,3,2,1,0:T(8,128)}, u32[]{:S(2)}) copy-start(f32[1,2,27,16,256]{4,3,2,1,0:T(8,128)} %param.9) | copy-start | bytes 2654212

commit v3 on v2

--- a/solution.py
+++ b/solution.py
@@ -273,8 +273,17 @@
                 sec_copy(3).start()
         pltpu.make_async_copy(upv.at[tick], up.at[tick], up_sem.at[tick]).start()
 
-    lane = lax.broadcasted_iota(jnp.int32, (block, VOX), 1)
-    ld, lh, lw = lane // PLANE, (lane // TW) % TH, lane % TW
+    lane = lax.broadcasted_iota(jnp.int32, (8, VOX), 1)
+    masks = {}
+    for step, size in ((1, TW), (TW, TH), (PLANE, TD)):
+        at_axis = (lane // step) % size
+        masks[step] = at_axis >= 1
+        masks[-step] = at_axis < size - 1
+
+    def moved(x, by):
+        if by == 0:
+            return x
+        return jnp.where(masks[by], pltpu.roll(x, by % VOX, 2), 0.0)
 
     def g_copy(b):
         return pltpu.make_async_remote_copy(
@@ -293,22 +302,20 @@
         d_to_mate(stage, 1 - core).wait_recv()
         arrive(stage)
 
-        @pl.loop(0, n)
+        @pl.loop(0, n // 2)
         def _(r):
-            x = d_recv[stage, lax.rem(r, 2), r // (2 * nz), lax.rem(r // 2, nz)].astype(jnp.float32)
-            cols = pl.ds(pl.multiple_of(r * VOX, VOX), VOX)
-            for tap in range(TAPS):
-                dd, dh, dw = tap_offset(tap)
-                flat = dd * PLANE + dh * TW + dw
-                s = x if flat == 0 else pltpu.roll(x, flat % VOX, 1)
-                ok = None
-                for c, by, size in ((ld, dd, TD), (lh, dh, TH), (lw, dw, TW)):
-                    if by:
-                        this = c >= 1 if by > 0 else c < size - 1
-                        ok = this if ok is None else ok & this
-                if ok is not None:
-                    s = jnp.where(ok, s, 0.0)
-                big[tap * block:(tap + 1) * block, cols] = s.astype(jnp.bfloat16)
+            yy, zz = r // nz, lax.rem(r, nz)
+            for cc in (0, 1):
+                x = d_recv[stage, cc, yy, zz].astype(jnp.float32).reshape(block // 8, 8, VOX)
+                cols = pl.ds(pl.multiple_of((2 * r + cc) * VOX, VOX), VOX)
+                for dw in (-1, 0, 1):
+                    xw = moved(x, dw)
+                    for dh in (-1, 0, 1):
+                        xh = moved(xw, dh * TW)
+                        for dd in (-1, 0, 1):
+                            lo = (9 * (dd + 1) + 3 * (dh + 1) + dw + 1) * block
+                            s = moved(xh, dd * PLANE).reshape(block, VOX)
+                            big[lo:lo + block, cols] = s.astype(jnp.bfloat16)
 
         @pl.loop(0, tiles)
         def _(m):
@@ -365,7 +372,7 @@
             jax.ShapeDtypeStruct((TICKS, 4, VOX, channels), bf),
             jax.ShapeDtypeStruct((2, TAPS, block // 2, channels), f32),
         ),
-        in_specs=[pl.BlockSpec(memory_space=pltpu.SMEM), hbm, hbm, hbm],
+        in_specs=[pl.BlockSpec(memory_space=pltpu.SMEM)] + [pl.BlockSpec(memory_space=pltpu.HBM)] * 3,
         out_specs=(hbm, vm),
         scratch_shapes=[
             pltpu.VMEM(weights.shape[1:], bf),
@@ -392,7 +399,7 @@
             dma((stages,)), dma((stages,)), dma((2,)), dma((2,)),
         ],
         compiler_params=pltpu.CompilerParams(
-            collective_id=0, has_side_effects=True, vmem_limit_bytes=48 * 1024 * 1024),
+            collective_id=0, has_side_effects=True, vmem_limit_bytes=63 * 1024 * 1024),
         cost_estimate=pl.CostEstimate(flops=12 * TICKS * VOX * TAPS * channels * channels,
                                       bytes_accessed=weights.size * 2, transcendentals=0),
     )(plan, incoming, feed, weights)

time: 59.6 us -> 61.5 us (1.032)
  Pallas kernels: 54.1 us -> 55.8 us
  other arithmetic: 1.1 us -> 2.27 us
  local copies, waits for them, and re-layouts: 2.96 us -> 1.87 us
    pallas_call x1, Pallas kernels: 54.1 us -> 55.8 us  [body(): pl.pallas_call(functools.partial(kernel, n, nsec), out_shape=(jax.ShapeDt...]
    broadcast_in_dim x1, other arithmetic: 1.1 us -> 2.27 us  [body(): return (up[:, None], new_momentum[None])]
    unnamed x7 -> x3, local copies, waits for them, and re-layouts: 2.96 us -> 1.87 us
where the time goes in v3:
time: 61.5 us; the launch traced here: 61.3 us
  Pallas kernels  55.8 us (91%)
  other arithmetic  2.27 us (4%)
  local copies, waits for them, and re-layouts  1.87 us (3%)
  between operations  1.3 us (2%)
    pallas_call x1, Pallas kernels, body(): pl.pallas_call(functools.partial(kernel, n, nsec), out_shape=(jax.ShapeDt...  55.8 us
    broadcast_in_dim x1, other arithmetic, body(): return (up[:, None], new_momentum[None])  2.27 us
    unnamed x3, local copies, waits for them, and re-layouts  1.87 us

profile of v3, /device:TPU:25, one launch (start us, length us, event | category | flops | bytes accessed | tf_op | source)
XLA Modules:
  0.0 61.3 jit_solution(2510456473161703468)
XLA Ops:
  1.3 0.0 copy-start
  1.3 55.8 %shard_map.68 = (bf16[2,4,128,256]{3,2,1,0:T(8,128)(2,1)}, f32[2,27,16,256]{3,2,1,0:T(8,128)}) custom-call(s32[1,1]{1,0:T(1,128)S(6)} %copy.9.plan, bf16[1,4,128,256]{3,2,1,0:T(8,128)(2,1)} %incoming.1, bf16[4,4,128,256]{3,2,1,0:T(8,128)(2,1)} %feed.1, bf16[1,2,27,256,256]{4,3,2,1,0:T(8,128)(2,1)} %weights.1), custom_call_target="tpu_custom_call" | custom-call | flops 5435817984 | bytes 7077888 | tf_op jit(solution)/shard_map/pallas_call | solution.py:369
  57.1 0.0 copy-done
  57.1 2.3 %fusion = f32[1,2,27,16,256]{4,3,2,1,0:T(8,128)} fusion(f32[2,27,16,256]{3,2,1,0:T(8,128)} %get-tuple-element.5, f32[1,2,27,16,256]{4,3,2,1,0:T(8,128)S(1)} %copy-done), kind=kLoop, calls=%fused_computation.1 | loop fusion | flops 663552 | bytes 2654208 | tf_op jit(solution)/shard_map/broadcast_in_dim | solution.py:407
  59.4 1.9 %copy.10 = bf16[2,1,4,128,256]{4,3,2,1,0:T(8,128)(2,1)} copy(bf16[2,1,4,128,256]{4,3,2,1,0:T(8,128)(2,1)} %bitcast.9) | data formatting | bytes 1048576
Async XLA Ops:
  1.3 55.8 %copy-start = (f32[1,2,27,16,256]{4,3,2,1,0:T(8,128)S(1)}, f32[1,2,27,16,256]{4,3,2,1,0:T(8,128)}, u32[]{:S(2)}) copy-start(f32[1,2,27,16,256]{4,3,2,1,0:T(8,128)} %param.9) | copy-start | bytes 2654212

commit v4 on v3

--- a/solution.py
+++ b/solution.py
@@ -56,8 +56,8 @@
 
 
 def kernel(n, nsec, plan, incoming, feed, weights, up, grad,
-           w_ref, first, pool, nxt, upv, ea, oa, eb, ob, a_send, d_send, d_mid, a_recv, d_recv, big, acc,
-           g_send, g_recv, w_sem, in_sem, up_sem, sec_s, sec_r, as_s, as_r, ar_s, ar_r,
+           w_ref, w_cat, cols, first, pool, nxt, upv, ea, oa, eb, ob, a_send, d_send, d_mid, a_recv, d_recv, big, acc,
+           g_send, g_recv, w_sem, wc_sem, in_sem, up_sem, sec_s, sec_r, as_s, as_r, ar_s, ar_r,
            dz_s, dz_r, dy_s, dy_r, dm_s, dm_r, g_s, g_r):
     me = lax.axis_index("dp")
     sec = lax.axis_index("section")
@@ -83,7 +83,16 @@
     load_pool = pltpu.make_async_copy(feed, pool, in_sem.at[1])
     loads = [pltpu.make_async_copy(weights.at[0, b], w_ref.at[b], w_sem.at[b]) for b in (0, 1)]
     load_in.start()
+    channels = w_ref.shape[-1]
+
+    def load_cat(b):
+        for tap in range(TAPS):
+            pltpu.make_async_copy(weights.at[0, b, tap], w_cat.at[b, :, tap * channels:(tap + 1) * channels],
+                                  wc_sem.at[b]).start()
+
+    load_cat(1)
     loads[1].start()
+    load_cat(0)
     loads[0].start()
     load_pool.start()
 
@@ -201,16 +210,19 @@
                 a_relay(stage, y_of(j), (y, z_of(k))).wait_send()
         d_to_mate(stage, core).wait_send()
 
+    def gather(even, odd, flip):
+        for tap in range(TAPS):
+            lo = tap * channels
+            cols[:, lo:lo + channels] = patch(even, odd, TAPS - 1 - tap if flip else tap)
+
     def convs(b, hook):
-        fwd = jnp.zeros((VOX, w_ref.shape[2]), jnp.float32)
-        for tap in range(TAPS):
-            fwd += lax.dot_general(patch(ea, oa, tap), w_ref[b, tap], (((1,), (1,)), ((), ())),
-                                   preferred_element_type=jnp.float32)
+        gather(ea, oa, False)
+        fwd = lax.dot_general(cols[...], w_cat[b], (((1,), (1,)), ((), ())),
+                              preferred_element_type=jnp.float32)
         hook()
-        bwd = jnp.zeros((VOX, w_ref.shape[3]), jnp.float32)
-        for tap in range(TAPS):
-            bwd += jnp.dot(patch(eb, ob, TAPS - 1 - tap), w_ref[b, tap],
-                           preferred_element_type=jnp.float32)
+        gather(eb, ob, True)
+        bwd = jnp.dot(cols[...], w_ref[b].reshape(TAPS * channels, channels),
+                      preferred_element_type=jnp.float32)
         return fwd, bwd
 
     def sec_copy(j):
@@ -242,6 +254,7 @@
         fill(eb, ob, dy2)
         if tick == 0:
             loads[1].wait()
+            pltpu.make_async_copy(w_cat.at[1], w_cat.at[1], wc_sem.at[1]).wait()
         fwd, bwd = convs(1, lambda: relay(2 * tick - 1) if tick else None)
         x2 = (cur[1].astype(jnp.float32) - fwd).astype(jnp.bfloat16)
         dx1 = (cur[2].astype(jnp.float32) + bwd * silu_grad(y1, s1)).astype(jnp.bfloat16)
@@ -261,6 +274,7 @@
         fill(eb, ob, e1)
         if tick == 0:
             loads[0].wait()
+            pltpu.make_async_copy(w_cat.at[0], w_cat.at[0], wc_sem.at[0]).wait()
         fwd, bwd = convs(0, lambda: relay(2 * tick))
         u = upv[tick, 1].astype(jnp.float32)
         s2 = sigmoid(u)
@@ -366,6 +380,8 @@
     vm = pl.BlockSpec(memory_space=pltpu.VMEM)
     hbm = pl.BlockSpec(memory_space=pl.ANY)
     dma = pltpu.SemaphoreType.DMA
+    incoming = pltpu.with_memory_space_constraint(incoming, pltpu.HBM)
+    feed = pltpu.with_memory_space_constraint(feed, pltpu.HBM)
     up, grad = pl.pallas_call(
         functools.partial(kernel, n, nsec),
         out_shape=(
@@ -376,6 +392,8 @@
         out_specs=(hbm, vm),
         scratch_shapes=[
             pltpu.VMEM(weights.shape[1:], bf),
+            pltpu.VMEM((2, channels, TAPS * channels), bf),
+            pltpu.VMEM((VOX, TAPS * channels), bf),
             pltpu.VMEM((4, VOX, channels), bf),
             pltpu.VMEM(feed.shape, bf),
             pltpu.VMEM((4, VOX, channels), bf),
@@ -393,13 +411,13 @@
             pltpu.VMEM((2, TAPS * block, LANES), f32),
             pltpu.VMEM((2, TAPS, block // 2, LANES), f32),
             pltpu.VMEM((2, TAPS, block // 2, LANES), f32),
-            dma((2,)), dma((2,)), dma((TICKS,)), dma((4,)), dma((4,)),
+            dma((2,)), dma((2,)), dma((2,)), dma((TICKS,)), dma((4,)), dma((4,)),
             dma((stages, 2 * (ny + nz))), dma((stages, ny, nz, 2)), dma((stages, ny, nz)), dma((stages, ny, nz)),
             dma((stages, nz)), dma((stages, nz)), dma((stages, ny)), dma((stages, ny)),
             dma((stages,)), dma((stages,)), dma((2,)), dma((2,)),
         ],
         compiler_params=pltpu.CompilerParams(
-            collective_id=0, has_side_effects=True, vmem_limit_bytes=63 * 1024 * 1024),
+            collective_id=0, has_side_effects=True, vmem_limit_bytes=48 * 1024 * 1024),
         cost_estimate=pl.CostEstimate(flops=12 * TICKS * VOX * TAPS * channels * channels,
                                       bytes_accessed=weights.size * 2, transcendentals=0),
     )(plan, incoming, feed, weights)

time: 61.5 us -> 59.9 us (0.974)
  the two profiles are of different devices: /device:TPU:25 before, /device:TPU:0 now
where the time goes in v4:
time: 59.9 us; the launch traced here: 58.8 us
  Pallas kernels  55.6 us (93%)
  between operations  1.3 us (2%)
  other arithmetic  1.1 us (2%)
  local copies, waits for them, and re-layouts  0.8 us (1%)
    pallas_call x1, Pallas kernels, body(): pl.pallas_call(functools.partial(kernel, n, nsec), out_shape=(jax.ShapeDt...  55.6 us

profile of v4, /device:TPU:0, one launch (start us, length us, event | category | flops | bytes accessed | tf_op | source)
XLA Modules:
  0.0 58.8 jit_solution(7847549997087003953)
XLA Ops:
  1.3 0.0 copy-start
  1.3 55.6 %shard_map.68 = (bf16[2,4,128,256]{3,2,1,0:T(8,128)(2,1)S(1)}, f32[2,27,16,256]{3,2,1,0:T(8,128)S(1)}) custom-call(s32[1,1]{1,0:T(1,128)S(6)} %copy.9.plan, bf16[1,4,128,256]{3,2,1,0:T(8,128)(2,1)} %incoming.1, bf16[4,4,128,256]{3,2,1,0:T(8,128)(2,1)} %feed.1, bf16[1,2,27,256,256]{4,3,2,1,0:T(8,128)(2,1)} %weights.1), custom_call_target="tpu_custom_call" | custom-call | flops 5435817984 | bytes 7077888 | tf_op jit(solution)/shard_map/pallas_call | solution.py:385
  56.8 0.0 copy-done
  56.9 1.1 %fusion = f32[1,2,27,16,256]{4,3,2,1,0:T(8,128)} fusion(f32[2,27,16,256]{3,2,1,0:T(8,128)S(1)} %get-tuple-element.5, f32[1,2,27,16,256]{4,3,2,1,0:T(8,128)S(1)} %copy-done), kind=kLoop, calls=%fused_computation.1 | loop fusion | flops 663552 | bytes 2654208 | tf_op jit(solution)/shard_map/broadcast_in_dim | solution.py:425
  58.0 0.8 %copy.10 = bf16[2,1,4,128,256]{4,3,2,1,0:T(8,128)(2,1)} copy(bf16[2,1,4,128,256]{4,3,2,1,0:T(8,128)(2,1)S(1)} %bitcast.9) | data formatting | bytes 1048576
Async XLA Ops:
  1.3 55.6 %copy-start = (f32[1,2,27,16,256]{4,3,2,1,0:T(8,128)S(1)}, f32[1,2,27,16,256]{4,3,2,1,0:T(8,128)}, u32[]{:S(2)}) copy-start(f32[1,2,27,16,256]{4,3,2,1,0:T(8,128)} %param.9) | copy-start | bytes 2654212

commit v5 on v3

--- a/solution.py
+++ b/solution.py
@@ -16,10 +16,6 @@
 TAPS = 27
 LANES = 128
 MESH = pl.DeviceIdType.MESH
-
-
-def tap_offset(tap):
-    return tap // 9 - 1, (tap // 3) % 3 - 1, tap % 3 - 1
 
 
 def sigmoid(u):
@@ -45,18 +41,18 @@
             even[wi, d + 1] = jnp.concatenate([edge, plane, edge], 0).astype(jnp.bfloat16)
 
 
-def patch(even, odd, tap):
-    dd, dh, dw = tap_offset(tap)
+def patch(even, odd, depth, tap):
+    dh, dw = tap // 3 - 1, tap % 3 - 1
     if dh == 0:
-        cut = odd[dw + 1, dd + 1:dd + 1 + TD]
+        cut = odd[dw + 1, pl.ds(depth, TD)]
     else:
         lo = (dh + 1) * TW
-        cut = even[dw + 1, dd + 1:dd + 1 + TD, lo:lo + PLANE]
+        cut = even[dw + 1, pl.ds(depth, TD), lo:lo + PLANE]
     return cut.reshape(VOX, cut.shape[-1])
 
 
 def kernel(n, nsec, plan, incoming, feed, weights, up, grad,
-           w_ref, first, pool, nxt, upv, ea, oa, eb, ob, a_send, d_send, d_mid, a_recv, d_recv, big, acc,
+           w_ref, pool, upv, ea, oa, eb, ob, a_send, d_send, d_mid, a_recv, d_recv, big, acc,
            g_send, g_recv, w_sem, in_sem, up_sem, sec_s, sec_r, as_s, as_r, ar_s, ar_r,
            dz_s, dz_r, dy_s, dy_r, dm_s, dm_r, g_s, g_r):
     me = lax.axis_index("dp")
@@ -79,7 +75,10 @@
     def y_of(k):
         return lax.rem(y + k, ny)
 
-    load_in = pltpu.make_async_copy(incoming.at[0], first, in_sem.at[0])
+    def up_copy(tick):
+        return pltpu.make_async_copy(upv.at[tick], up.at[tick], up_sem.at[tick])
+
+    load_in = pltpu.make_async_copy(incoming.at[0], upv.at[0], in_sem.at[0])
     load_pool = pltpu.make_async_copy(feed, pool, in_sem.at[1])
     loads = [pltpu.make_async_copy(weights.at[0, b], w_ref.at[b], w_sem.at[b]) for b in (0, 1)]
     load_in.start()
@@ -202,76 +201,83 @@
         d_to_mate(stage, core).wait_send()
 
     def convs(b, hook):
-        fwd = jnp.zeros((VOX, w_ref.shape[2]), jnp.float32)
-        for tap in range(TAPS):
-            fwd += lax.dot_general(patch(ea, oa, tap), w_ref[b, tap], (((1,), (1,)), ((), ())),
-                                   preferred_element_type=jnp.float32)
+        zero = jnp.zeros((VOX, w_ref.shape[2]), jnp.float32)
+
+        def forward(dd, total):
+            for tap in range(9):
+                total += lax.dot_general(patch(ea, oa, dd, tap), w_ref[b, 9 * dd + tap],
+                                         (((1,), (1,)), ((), ())), preferred_element_type=jnp.float32)
+            return total
+
+        def backward(dd, total):
+            for tap in range(9):
+                total += jnp.dot(patch(eb, ob, 2 - dd, 8 - tap), w_ref[b, 9 * dd + tap],
+                                 preferred_element_type=jnp.float32)
+            return total
+
+        fwd = lax.fori_loop(0, 3, forward, zero)
         hook()
-        bwd = jnp.zeros((VOX, w_ref.shape[3]), jnp.float32)
-        for tap in range(TAPS):
-            bwd += jnp.dot(patch(eb, ob, TAPS - 1 - tap), w_ref[b, tap],
-                           preferred_element_type=jnp.float32)
+        bwd = lax.fori_loop(0, 3, backward, zero)
         return fwd, bwd
 
     def sec_copy(j):
         return pltpu.make_async_remote_copy(
-            src_ref=upv.at[0, j], dst_ref=nxt.at[j], send_sem=sec_s.at[j], recv_sem=sec_r.at[j],
+            src_ref=upv.at[0, j], dst_ref=upv.at[1, j], send_sem=sec_s.at[j], recv_sem=sec_r.at[j],
             device_id={"section": lax.rem(sec + nsec - 1, nsec)}, device_id_type=MESH)
 
-    for tick in range(TICKS):
-        if tick == 0:
-            cur = first
-        else:
-            cur = nxt
+    stages = 2 * TICKS
+
+    @pl.loop(0, stages)
+    def _(stage):
+        tick, p = stage // 2, lax.rem(stage, 2)
+
+        @pl.when(stage == 2)
+        def _():
             load_pool.wait()
 
             @pl.when(last)
             def _():
-                nxt[...] = pool[plan[0, 0]]
+                upv[1] = pool[plan[0, 0]]
 
             @pl.when(sec < nsec - 1)
             def _():
                 for j in range(4):
                     sec_copy(j).wait_recv()
-        y1 = cur[0].astype(jnp.float32)
-        s1 = sigmoid(y1)
-        a1 = y1 * s1
-        dy2 = cur[3].astype(jnp.float32)
-        share(2 * tick, a1.astype(jnp.bfloat16), dy2)
-        fill(ea, oa, a1)
-        fill(eb, ob, dy2)
-        if tick == 0:
-            loads[1].wait()
-        fwd, bwd = convs(1, lambda: relay(2 * tick - 1) if tick else None)
-        x2 = (cur[1].astype(jnp.float32) - fwd).astype(jnp.bfloat16)
-        dx1 = (cur[2].astype(jnp.float32) + bwd * silu_grad(y1, s1)).astype(jnp.bfloat16)
-        upv[tick, 1] = x2
-        upv[tick, 2] = dx1
-        if tick == 0:
-            @pl.when(sec > 0)
-            def _():
-                sec_copy(1).start()
-                sec_copy(2).start()
-        u = x2.astype(jnp.float32)
-        s2 = sigmoid(u)
-        a2 = u * s2
-        e1 = dx1.astype(jnp.float32)
-        share(2 * tick + 1, a2.astype(jnp.bfloat16), e1)
-        fill(ea, oa, a2)
-        fill(eb, ob, e1)
-        if tick == 0:
-            loads[0].wait()
-        fwd, bwd = convs(0, lambda: relay(2 * tick))
-        u = upv[tick, 1].astype(jnp.float32)
-        s2 = sigmoid(u)
-        upv[tick, 0] = (cur[0].astype(jnp.float32) - fwd).astype(jnp.bfloat16)
-        upv[tick, 3] = (cur[3].astype(jnp.float32) + bwd * silu_grad(u, s2)).astype(jnp.bfloat16)
-        if tick == 0:
-            @pl.when(sec > 0)
-            def _():
-                sec_copy(0).start()
-                sec_copy(3).start()
-        pltpu.make_async_copy(upv.at[tick], up.at[tick], up_sem.at[tick]).start()
+
+        u = upv[tick, p].astype(jnp.float32)
+        act = u * sigmoid(u)
+        err = upv[tick, 3 - p].astype(jnp.float32)
+        share(stage, act.astype(jnp.bfloat16), err)
+        fill(ea, oa, act)
+        fill(eb, ob, err)
+        for b in (0, 1):
+            @pl.when(stage == 1 - b)
+            def _():
+                loads[b].wait()
+
+        def hook():
+            @pl.when(stage > 0)
+            def _():
+                relay(stage - 1)
+
+        fwd, bwd = convs(1 - p, hook)
+        u = upv[tick, p].astype(jnp.float32)
+        upv[tick, 1 - p] = (upv[tick, 1 - p].astype(jnp.float32) - fwd).astype(jnp.bfloat16)
+        upv[tick, 2 + p] = (upv[tick, 2 + p].astype(jnp.float32) + bwd * silu_grad(u, sigmoid(u))).astype(jnp.bfloat16)
+
+        @pl.when((stage == 0) & (sec > 0))
+        def _():
+            sec_copy(1).start()
+            sec_copy(2).start()
+
+        @pl.when((stage == 1) & (sec > 0))
+        def _():
+            sec_copy(0).start()
+            sec_copy(3).start()
+
+        @pl.when(p == 1)
+        def _():
+            up_copy(tick).start()
 
     lane = lax.broadcasted_iota(jnp.int32, (8, VOX), 1)
     masks = {}
@@ -292,46 +298,54 @@
 
     tiles = 3
     per = TAPS * block // tiles
-    stages = 2 * TICKS
     relay(stages - 1)
     swap_errors(0)
-    for stage in range(stages):
-        b = stage % 2
-        if stage + 1 < stages:
+    @pl.loop(0, stages)
+    def _(stage):
+        b = lax.rem(stage, 2)
+
+        @pl.when(stage + 1 < stages)
+        def _():
             swap_errors(stage + 1)
+
         d_to_mate(stage, 1 - core).wait_recv()
         arrive(stage)
 
-        @pl.loop(0, n // 2)
+        @pl.loop(0, n)
         def _(r):
-            yy, zz = r // nz, lax.rem(r, nz)
-            for cc in (0, 1):
-                x = d_recv[stage, cc, yy, zz].astype(jnp.float32).reshape(block // 8, 8, VOX)
-                cols = pl.ds(pl.multiple_of((2 * r + cc) * VOX, VOX), VOX)
-                for dw in (-1, 0, 1):
-                    xw = moved(x, dw)
-                    for dh in (-1, 0, 1):
-                        xh = moved(xw, dh * TW)
-                        for dd in (-1, 0, 1):
-                            lo = (9 * (dd + 1) + 3 * (dh + 1) + dw + 1) * block
-                            s = moved(xh, dd * PLANE).reshape(block, VOX)
-                            big[lo:lo + block, cols] = s.astype(jnp.bfloat16)
+            q = r // 2
+            x = d_recv[stage, lax.rem(r, 2), q // nz, lax.rem(q, nz)]
+            x = x.astype(jnp.float32).reshape(block // 8, 8, VOX)
+            cols = pl.ds(pl.multiple_of(r * VOX, VOX), VOX)
+            for dw in (-1, 0, 1):
+                xw = moved(x, dw)
+                for dh in (-1, 0, 1):
+                    xh = moved(xw, dh * TW)
+                    for dd in (-1, 0, 1):
+                        lo = (9 * (dd + 1) + 3 * (dh + 1) + dw + 1) * block
+                        s = moved(xh, dd * PLANE).reshape(block, VOX)
+                        big[lo:lo + block, cols] = s.astype(jnp.bfloat16)
 
         @pl.loop(0, tiles)
         def _(m):
             rows = pl.ds(pl.multiple_of(m * per, 16), per)
             got = jnp.dot(big[rows, :], a_recv[stage].reshape(n * VOX, LANES),
                           preferred_element_type=jnp.float32)
-            if stage < 2:
+            @pl.when(stage < 2)
+            def _():
                 acc[b, rows, :] = got
-            else:
+
+            @pl.when(stage >= 2)
+            def _():
                 acc[b, rows, :] += got
-        if stage >= 2 * TICKS - 2:
-            view = acc.at[b]
+
+        @pl.when(stage >= stages - 2)
+        def _():
+            lo = pl.multiple_of((1 - core) * half, 8)
             for tap in range(TAPS):
-                lo = pl.multiple_of(tap * block + (1 - core) * half, 8)
-                g_send[b, tap] = view[pl.ds(lo, half), :]
+                g_send[b, tap] = acc[b, pl.ds(tap * block + lo, half), :]
             g_copy(b).start()
+
     mine = pl.ds(pl.multiple_of(core * LANES, LANES), LANES)
     other = pl.ds(pl.multiple_of((1 - core) * LANES, LANES), LANES)
     for b in (0, 1):
@@ -343,10 +357,12 @@
         grad[1 - b, :, :, other] = g_recv[b]
     for b in (0, 1):
         g_copy(b).wait_send()
-    for stage in range(stages):
+    @pl.loop(0, stages)
+    def _(stage):
         sent(stage)
+
     for tick in range(TICKS):
-        pltpu.make_async_copy(upv.at[tick], up.at[tick], up_sem.at[tick]).wait()
+        up_copy(tick).wait()
 
     @pl.when(sec > 0)
     def _():
@@ -366,6 +382,8 @@
     vm = pl.BlockSpec(memory_space=pltpu.VMEM)
     hbm = pl.BlockSpec(memory_space=pl.ANY)
     dma = pltpu.SemaphoreType.DMA
+    incoming = pltpu.with_memory_space_constraint(incoming, pltpu.HBM)
+    feed = pltpu.with_memory_space_constraint(feed, pltpu.HBM)
     up, grad = pl.pallas_call(
         functools.partial(kernel, n, nsec),
         out_shape=(
@@ -376,9 +394,7 @@
         out_specs=(hbm, vm),
         scratch_shapes=[
             pltpu.VMEM(weights.shape[1:], bf),
-            pltpu.VMEM((4, VOX, channels), bf),
             pltpu.VMEM(feed.shape, bf),
-            pltpu.VMEM((4, VOX, channels), bf),
             pltpu.VMEM((TICKS, 4, VOX, channels), bf),
             pltpu.VMEM((3, TD + 2, PLANE + 2 * TW, channels), bf),
             pltpu.VMEM((3, TD + 2, PLANE, channels), bf),
@@ -399,7 +415,7 @@
             dma((stages,)), dma((stages,)), dma((2,)), dma((2,)),
         ],
         compiler_params=pltpu.CompilerParams(
-            collective_id=0, has_side_effects=True, vmem_limit_bytes=63 * 1024 * 1024),
+            collective_id=0, has_side_effects=True, vmem_limit_bytes=48 * 1024 * 1024),
         cost_estimate=pl.CostEstimate(flops=12 * TICKS * VOX * TAPS * channels * channels,
                                       bytes_accessed=weights.size * 2, transcendentals=0),
     )(plan, incoming, feed, weights)

time: 61.5 us -> 64 us (1.041)
  the two profiles are of different devices: /device:TPU:25 before, /device:TPU:0 now
where the time goes in v5:
time: 64 us; the launch traced here: 62.9 us
  Pallas kernels  59.7 us (93%)
  between operations  1.3 us (2%)
  other arithmetic  1.1 us (2%)
  local copies, waits for them, and re-layouts  0.8 us (1%)
    pallas_call x1, Pallas kernels, body(): pl.pallas_call(functools.partial(kernel, n, nsec), out_shape=(jax.ShapeDt...  59.7 us

profile of v5, /device:TPU:0, one launch (start us, length us, event | category | flops | bytes accessed | tf_op | source)
XLA Modules:
  0.0 62.9 jit_solution(14048806788076783813)
XLA Ops:
  1.3 0.0 copy-start
  1.3 59.7 %shard_map.68 = (bf16[2,4,128,256]{3,2,1,0:T(8,128)(2,1)S(1)}, f32[2,27,16,256]{3,2,1,0:T(8,128)S(1)}) custom-call(s32[1,1]{1,0:T(1,128)S(6)} %copy.9.plan, bf16[1,4,128,256]{3,2,1,0:T(8,128)(2,1)} %incoming.1, bf16[4,4,128,256]{3,2,1,0:T(8,128)(2,1)} %feed.1, bf16[1,2,27,256,256]{4,3,2,1,0:T(8,128)(2,1)} %weights.1), custom_call_target="tpu_custom_call" | custom-call | flops 5435817984 | bytes 7077888 | tf_op jit(solution)/shard_map/pallas_call | solution.py:387
  61.0 0.0 copy-done
  61.0 1.1 %fusion = f32[1,2,27,16,256]{4,3,2,1,0:T(8,128)} fusion(f32[2,27,16,256]{3,2,1,0:T(8,128)S(1)} %get-tuple-element.5, f32[1,2,27,16,256]{4,3,2,1,0:T(8,128)S(1)} %copy-done), kind=kLoop, calls=%fused_computation.1 | loop fusion | flops 663552 | bytes 2654208 | tf_op jit(solution)/shard_map/broadcast_in_dim | solution.py:423
  62.1 0.8 %copy.10 = bf16[2,1,4,128,256]{4,3,2,1,0:T(8,128)(2,1)} copy(bf16[2,1,4,128,256]{4,3,2,1,0:T(8,128)(2,1)S(1)} %bitcast.9) | data formatting | bytes 1048576
Async XLA Ops:
  1.3 59.7 %copy-start = (f32[1,2,27,16,256]{4,3,2,1,0:T(8,128)S(1)}, f32[1,2,27,16,256]{4,3,2,1,0:T(8,128)}, u32[]{:S(2)}) copy-start(f32[1,2,27,16,256]{4,3,2,1,0:T(8,128)} %param.9) | copy-start | bytes 2654212

commit v6 on v3

--- a/solution.py
+++ b/solution.py
@@ -57,7 +57,7 @@
 
 def kernel(n, nsec, plan, incoming, feed, weights, up, grad,
            w_ref, first, pool, nxt, upv, ea, oa, eb, ob, a_send, d_send, d_mid, a_recv, d_recv, big, acc,
-           g_send, g_recv, w_sem, in_sem, up_sem, sec_s, sec_r, as_s, as_r, ar_s, ar_r,
+           g_send, g_recv, w_sem, in_sem, up_sem, sec_s, sec_r, as_s, as_r, ar_s, ar_r, ap_s, ap_r,
            dz_s, dz_r, dy_s, dy_r, dm_s, dm_r, g_s, g_r):
     me = lax.axis_index("dp")
     sec = lax.axis_index("section")
@@ -74,7 +74,10 @@
         return (zz * ny + yy) * 2 + cc
 
     def z_of(k):
-        return lax.rem(z + k, nz)
+        low, high = lax.rem(z, 2), z // 2
+        low = 1 - low if k % 2 else low
+        high = 1 - high if k // 2 else high
+        return 2 * high + low
 
     def y_of(k):
         return lax.rem(y + k, ny)
@@ -143,7 +146,7 @@
     def directs(stage):
         mine = (y, z, core)
         out = []
-        for k in range(1, nz):
+        for k in (1, 2):
             for cc in (0, 1):
                 out.append(a_direct(stage, len(out), at(z_of(k), y, cc), cc, mine))
         for k in range(1, ny):
@@ -165,17 +168,32 @@
         for yy in range(ny):
             d_mid[stage, yy, z] = d_send[stage, z, yy]
 
-    def relay(stage):
+    def pass_on(stage, slot):
+        return pltpu.make_async_remote_copy(
+            src_ref=a_recv.at[stage, y, slot], dst_ref=a_recv.at[stage, y, slot],
+            send_sem=ap_s.at[stage], recv_sem=ap_r.at[stage],
+            device_id={"dp": at(z_of(1), y, core)}, device_id_type=MESH)
+
+    def relay_near(stage):
+        for cc in (0, 1):
+            a_direct(stage, 0, mate, 0, (y, z_of(2), cc)).wait_recv()
+        pass_on(stage, z_of(2)).start()
+        for j in range(1, ny):
+            a_relay(stage, y_of(j), (y, z_of(2))).start()
+        for cc in (0, 1):
+            a_direct(stage, 0, mate, 0, (y, z_of(1), cc)).wait_recv()
+        for j in range(1, ny):
+            a_relay(stage, y_of(j), (y, z_of(1))).start()
+
+    def relay_far(stage):
         for k in range(1, nz):
             d_along_z(stage, z, z_of(k)).wait_recv()
         for k in range(1, ny):
             d_along_y(stage, y_of(k), y).start()
         d_recv[stage, core, y] = d_mid[stage, y]
-        for k in range(1, nz):
-            for cc in (0, 1):
-                a_direct(stage, 0, mate, 0, (y, z_of(k), cc)).wait_recv()
-            for j in range(1, ny):
-                a_relay(stage, y_of(j), (y, z_of(k))).start()
+        pass_on(stage, z_of(3)).wait_recv()
+        for j in range(1, ny):
+            a_relay(stage, y_of(j), (y, z_of(3))).start()
 
     def swap_errors(stage):
         for k in range(1, ny):
@@ -199,14 +217,16 @@
             d_along_y(stage, y_of(j), y).wait_send()
             for k in range(1, nz):
                 a_relay(stage, y_of(j), (y, z_of(k))).wait_send()
+        pass_on(stage, z_of(2)).wait_send()
         d_to_mate(stage, core).wait_send()
 
-    def convs(b, hook):
+    def convs(b, near, far):
+        near()
         fwd = jnp.zeros((VOX, w_ref.shape[2]), jnp.float32)
         for tap in range(TAPS):
             fwd += lax.dot_general(patch(ea, oa, tap), w_ref[b, tap], (((1,), (1,)), ((), ())),
                                    preferred_element_type=jnp.float32)
-        hook()
+        far()
         bwd = jnp.zeros((VOX, w_ref.shape[3]), jnp.float32)
         for tap in range(TAPS):
             bwd += jnp.dot(patch(eb, ob, TAPS - 1 - tap), w_ref[b, tap],
@@ -242,7 +262,7 @@
         fill(eb, ob, dy2)
         if tick == 0:
             loads[1].wait()
-        fwd, bwd = convs(1, lambda: relay(2 * tick - 1) if tick else None)
+        fwd, bwd = convs(1, lambda: relay_near(1) if tick else None, lambda: relay_far(1) if tick else None)
         x2 = (cur[1].astype(jnp.float32) - fwd).astype(jnp.bfloat16)
         dx1 = (cur[2].astype(jnp.float32) + bwd * silu_grad(y1, s1)).astype(jnp.bfloat16)
         upv[tick, 1] = x2
@@ -261,7 +281,7 @@
         fill(eb, ob, e1)
         if tick == 0:
             loads[0].wait()
-        fwd, bwd = convs(0, lambda: relay(2 * tick))
+        fwd, bwd = convs(0, lambda: relay_near(2 * tick), lambda: relay_far(2 * tick))
         u = upv[tick, 1].astype(jnp.float32)
         s2 = sigmoid(u)
         upv[tick, 0] = (cur[0].astype(jnp.float32) - fwd).astype(jnp.bfloat16)
@@ -293,10 +313,12 @@
     tiles = 3
     per = TAPS * block // tiles
     stages = 2 * TICKS
-    relay(stages - 1)
+    relay_near(stages - 1)
     swap_errors(0)
     for stage in range(stages):
         b = stage % 2
+        if stage == 1:
+            relay_far(stages - 1)
         if stage + 1 < stages:
             swap_errors(stage + 1)
         d_to_mate(stage, 1 - core).wait_recv()
@@ -343,8 +365,10 @@
         grad[1 - b, :, :, other] = g_recv[b]
     for b in (0, 1):
         g_copy(b).wait_send()
-    for stage in range(stages):
+    @pl.loop(0, stages)
+    def _(stage):
         sent(stage)
+
     for tick in range(TICKS):
         pltpu.make_async_copy(upv.at[tick], up.at[tick], up_sem.at[tick]).wait()
 
@@ -366,6 +390,8 @@
     vm = pl.BlockSpec(memory_space=pltpu.VMEM)
     hbm = pl.BlockSpec(memory_space=pl.ANY)
     dma = pltpu.SemaphoreType.DMA
+    incoming = pltpu.with_memory_space_constraint(incoming, pltpu.HBM)
+    feed = pltpu.with_memory_space_constraint(feed, pltpu.HBM)
     up, grad = pl.pallas_call(
         functools.partial(kernel, n, nsec),
         out_shape=(
@@ -395,11 +421,12 @@
             pltpu.VMEM((2, TAPS, block // 2, LANES), f32),
             dma((2,)), dma((2,)), dma((TICKS,)), dma((4,)), dma((4,)),
             dma((stages, 2 * (ny + nz))), dma((stages, ny, nz, 2)), dma((stages, ny, nz)), dma((stages, ny, nz)),
+            dma((stages,)), dma((stages,)),
             dma((stages, nz)), dma((stages, nz)), dma((stages, ny)), dma((stages, ny)),
             dma((stages,)), dma((stages,)), dma((2,)), dma((2,)),
         ],
         compiler_params=pltpu.CompilerParams(
-            collective_id=0, has_side_effects=True, vmem_limit_bytes=63 * 1024 * 1024),
+            collective_id=0, has_side_effects=True, vmem_limit_bytes=48 * 1024 * 1024),
         cost_estimate=pl.CostEstimate(flops=12 * TICKS * VOX * TAPS * channels * channels,
                                       bytes_accessed=weights.size * 2, transcendentals=0),
     )(plan, incoming, feed, weights)

time: 61.5 us -> 60.6 us (0.985)
  the two profiles are of different devices: /device:TPU:25 before, /device:TPU:0 now
where the time goes in v6:
time: 60.6 us; the launch traced here: 60.4 us
  Pallas kernels  57.2 us (94%)
  between operations  1.3 us (2%)
  other arithmetic  1.1 us (2%)
  local copies, waits for them, and re-layouts  0.8 us (1%)
    pallas_call x1, Pallas kernels, body(): pl.pallas_call(functools.partial(kernel, n, nsec), out_shape=(jax.ShapeDt...  57.2 us

profile of v6, /device:TPU:0, one launch (start us, length us, event | category | flops | bytes accessed | tf_op | source)
XLA Modules:
  0.0 60.4 jit_solution(15756284750978887306)
XLA Ops:
  1.3 0.0 copy-start
  1.3 57.2 %shard_map.68 = (bf16[2,4,128,256]{3,2,1,0:T(8,128)(2,1)S(1)}, f32[2,27,16,256]{3,2,1,0:T(8,128)S(1)}) custom-call(s32[1,1]{1,0:T(1,128)S(6)} %copy.9.plan, bf16[1,4,128,256]{3,2,1,0:T(8,128)(2,1)} %incoming.1, bf16[4,4,128,256]{3,2,1,0:T(8,128)(2,1)} %feed.1, bf16[1,2,27,256,256]{4,3,2,1,0:T(8,128)(2,1)} %weights.1), custom_call_target="tpu_custom_call" | custom-call | flops 5435817984 | bytes 7077888 | tf_op jit(solution)/shard_map/pallas_call | solution.py:395
  58.5 0.0 copy-done
  58.5 1.1 %fusion = f32[1,2,27,16,256]{4,3,2,1,0:T(8,128)} fusion(f32[2,27,16,256]{3,2,1,0:T(8,128)S(1)} %get-tuple-element.5, f32[1,2,27,16,256]{4,3,2,1,0:T(8,128)S(1)} %copy-done), kind=kLoop, calls=%fused_computation.1 | loop fusion | flops 663552 | bytes 2654208 | tf_op jit(solution)/shard_map/broadcast_in_dim | solution.py:434
  59.6 0.8 %copy.10 = bf16[2,1,4,128,256]{4,3,2,1,0:T(8,128)(2,1)} copy(bf16[2,1,4,128,256]{4,3,2,1,0:T(8,128)(2,1)S(1)} %bitcast.9) | data formatting | bytes 1048576
Async XLA Ops:
  1.3 57.2 %copy-start = (f32[1,2,27,16,256]{4,3,2,1,0:T(8,128)S(1)}, f32[1,2,27,16,256]{4,3,2,1,0:T(8,128)}, u32[]{:S(2)}) copy-start(f32[1,2,27,16,256]{4,3,2,1,0:T(8,128)} %param.9) | copy-start | bytes 2654212

commit v7 on v6

--- a/solution.py
+++ b/solution.py
@@ -57,11 +57,11 @@
 
 def kernel(n, nsec, plan, incoming, feed, weights, up, grad,
            w_ref, first, pool, nxt, upv, ea, oa, eb, ob, a_send, d_send, d_mid, a_recv, d_recv, big, acc,
-           g_send, g_recv, w_sem, in_sem, up_sem, sec_s, sec_r, as_s, as_r, ar_s, ar_r, ap_s, ap_r,
-           dz_s, dz_r, dy_s, dy_r, dm_s, dm_r, g_s, g_r):
+           w_sem, in_sem, up_sem, sec_s, sec_r, as_s, as_r, ar_s, ar_r, ap_s, ap_r,
+           dz_s, dz_r, dy_s, dy_r, dm_s, dm_r, mp_s, mp_r):
     me = lax.axis_index("dp")
     sec = lax.axis_index("section")
-    ny, nz = a_recv.shape[1:3]
+    ny, nz = a_recv.shape[2:4]
     core = lax.rem(me, 2)
     y = lax.rem(me // 2, ny)
     z = me // (2 * ny)
@@ -115,13 +115,13 @@
 
     def a_direct(stage, idx, peer, to, slot):
         return pltpu.make_async_remote_copy(
-            src_ref=a_send.at[stage, to], dst_ref=a_recv.at[(stage,) + slot],
+            src_ref=a_send.at[stage, to], dst_ref=a_recv.at[(stage, to) + slot],
             send_sem=as_s.at[stage, idx], recv_sem=as_r.at[(stage,) + slot],
             device_id={"dp": peer}, device_id_type=MESH)
 
     def a_relay(stage, yy, slot):
         return pltpu.make_async_remote_copy(
-            src_ref=a_recv.at[(stage,) + slot], dst_ref=a_recv.at[(stage,) + slot],
+            src_ref=a_recv.at[(stage, core) + slot], dst_ref=a_recv.at[(stage, core) + slot],
             send_sem=ar_s.at[stage, yy, slot[1]], recv_sem=ar_r.at[(stage,) + slot],
             device_id={"dp": at(z, yy, core)}, device_id_type=MESH)
 
@@ -164,15 +164,21 @@
             d_along_z(stage, z_of(k), z).start()
         for copy in directs(stage):
             copy.start()
-        a_recv[stage, y, z, core] = a_send[stage, core]
+        a_recv[stage, core, y, z, core] = a_send[stage, core]
         for yy in range(ny):
             d_mid[stage, yy, z] = d_send[stage, z, yy]
 
     def pass_on(stage, slot):
         return pltpu.make_async_remote_copy(
-            src_ref=a_recv.at[stage, y, slot], dst_ref=a_recv.at[stage, y, slot],
+            src_ref=a_recv.at[stage, core, y, slot], dst_ref=a_recv.at[stage, core, y, slot],
             send_sem=ap_s.at[stage], recv_sem=ap_r.at[stage],
             device_id={"dp": at(z_of(1), y, core)}, device_id_type=MESH)
+
+    def a_to_mate(stage, whose, yy):
+        return pltpu.make_async_remote_copy(
+            src_ref=a_recv.at[stage, whose, yy], dst_ref=a_recv.at[stage, whose, yy],
+            send_sem=mp_s.at[stage, yy], recv_sem=mp_r.at[stage, yy],
+            device_id={"dp": mate}, device_id_type=MESH)
 
     def relay_near(stage):
         for cc in (0, 1):
@@ -194,6 +200,8 @@
         pass_on(stage, z_of(3)).wait_recv()
         for j in range(1, ny):
             a_relay(stage, y_of(j), (y, z_of(3))).start()
+        a_direct(stage, 0, mate, 0, (y, z, 1 - core)).wait_recv()
+        a_to_mate(stage, core, y).start()
 
     def swap_errors(stage):
         for k in range(1, ny):
@@ -201,12 +209,16 @@
         d_to_mate(stage, core).start()
 
     def arrive(stage):
-        a_direct(stage, 0, mate, 0, (y, z, 1 - core)).wait_recv()
         for j in range(1, ny):
             for cc in (0, 1):
                 a_direct(stage, 0, mate, 0, (y_of(j), z, cc)).wait_recv()
             for k in range(1, nz):
                 a_relay(stage, y, (y_of(j), z_of(k))).wait_recv()
+            a_to_mate(stage, core, y_of(j)).start()
+
+    def mate_arrives(stage):
+        for j in range(ny):
+            a_to_mate(stage, 1 - core, y_of(j)).wait_recv()
 
     def sent(stage):
         for k in range(1, nz):
@@ -218,6 +230,8 @@
             for k in range(1, nz):
                 a_relay(stage, y_of(j), (y, z_of(k))).wait_send()
         pass_on(stage, z_of(2)).wait_send()
+        for j in range(ny):
+            a_to_mate(stage, core, y_of(j)).wait_send()
         d_to_mate(stage, core).wait_send()
 
     def convs(b, near, far):
@@ -305,14 +319,8 @@
             return x
         return jnp.where(masks[by], pltpu.roll(x, by % VOX, 2), 0.0)
 
-    def g_copy(b):
-        return pltpu.make_async_remote_copy(
-            src_ref=g_send.at[b], dst_ref=g_recv.at[b], send_sem=g_s.at[b], recv_sem=g_r.at[b],
-            device_id={"dp": mate}, device_id_type=MESH)
-
-    tiles = 3
-    per = TAPS * block // tiles
     stages = 2 * TICKS
+    depth = n * VOX
     relay_near(stages - 1)
     swap_errors(0)
     for stage in range(stages):
@@ -328,43 +336,28 @@
         def _(r):
             yy, zz = r // nz, lax.rem(r, nz)
             for cc in (0, 1):
-                x = d_recv[stage, cc, yy, zz].astype(jnp.float32).reshape(block // 8, 8, VOX)
+                x = d_recv[stage, cc, yy, zz].astype(jnp.float32)
+                x = jnp.where(core == 0, x[:half], x[half:]).reshape(half // 8, 8, VOX)
                 cols = pl.ds(pl.multiple_of((2 * r + cc) * VOX, VOX), VOX)
+                rows = [None] * TAPS
                 for dw in (-1, 0, 1):
                     xw = moved(x, dw)
                     for dh in (-1, 0, 1):
                         xh = moved(xw, dh * TW)
                         for dd in (-1, 0, 1):
-                            lo = (9 * (dd + 1) + 3 * (dh + 1) + dw + 1) * block
-                            s = moved(xh, dd * PLANE).reshape(block, VOX)
-                            big[lo:lo + block, cols] = s.astype(jnp.bfloat16)
-
-        @pl.loop(0, tiles)
-        def _(m):
-            rows = pl.ds(pl.multiple_of(m * per, 16), per)
-            got = jnp.dot(big[rows, :], a_recv[stage].reshape(n * VOX, LANES),
-                          preferred_element_type=jnp.float32)
-            if stage < 2:
-                acc[b, rows, :] = got
-            else:
-                acc[b, rows, :] += got
-        if stage >= 2 * TICKS - 2:
-            view = acc.at[b]
-            for tap in range(TAPS):
-                lo = pl.multiple_of(tap * block + (1 - core) * half, 8)
-                g_send[b, tap] = view[pl.ds(lo, half), :]
-            g_copy(b).start()
-    mine = pl.ds(pl.multiple_of(core * LANES, LANES), LANES)
-    other = pl.ds(pl.multiple_of((1 - core) * LANES, LANES), LANES)
-    for b in (0, 1):
-        for tap in range(TAPS):
-            lo = pl.multiple_of(tap * block + core * half, 8)
-            grad[1 - b, tap, :, mine] = acc[b, pl.ds(lo, half), :]
-    for b in (0, 1):
-        g_copy(b).wait_recv()
-        grad[1 - b, :, :, other] = g_recv[b]
-    for b in (0, 1):
-        g_copy(b).wait_send()
+                            tap = 9 * (dd + 1) + 3 * (dh + 1) + dw + 1
+                            rows[tap] = moved(xh, dd * PLANE).reshape(half, VOX)
+                big[:, cols] = jnp.concatenate(rows, 0).astype(jnp.bfloat16)
+
+        mate_arrives(stage)
+        both = jnp.concatenate([a_recv[stage, 0].reshape(depth, LANES),
+                                a_recv[stage, 1].reshape(depth, LANES)], 1)
+        got = jnp.dot(big[...], both, preferred_element_type=jnp.float32)
+        if stage < 2:
+            acc[b] = got
+        else:
+            grad[1 - b] = (acc[b] + got).reshape(TAPS, half, 2 * LANES)
+
     @pl.loop(0, stages)
     def _(stage):
         sent(stage)
@@ -413,17 +406,15 @@
             pltpu.VMEM((stages, 2, VOX, LANES), bf),
             pltpu.VMEM((stages, nz, ny, block, VOX), bf),
             pltpu.VMEM((stages, ny, nz, block, VOX), bf),
-            pltpu.VMEM((stages, ny, nz, 2, VOX, LANES), bf),
+            pltpu.VMEM((stages, 2, ny, nz, 2, VOX, LANES), bf),
             pltpu.VMEM((stages, 2, ny, nz, block, VOX), bf),
-            pltpu.VMEM((TAPS * block, n * VOX), bf),
-            pltpu.VMEM((2, TAPS * block, LANES), f32),
-            pltpu.VMEM((2, TAPS, block // 2, LANES), f32),
-            pltpu.VMEM((2, TAPS, block // 2, LANES), f32),
+            pltpu.VMEM((TAPS * block // 2, n * VOX), bf),
+            pltpu.VMEM((2, TAPS * block // 2, channels), f32),
             dma((2,)), dma((2,)), dma((TICKS,)), dma((4,)), dma((4,)),
             dma((stages, 2 * (ny + nz))), dma((stages, ny, nz, 2)), dma((stages, ny, nz)), dma((stages, ny, nz)),
             dma((stages,)), dma((stages,)),
             dma((stages, nz)), dma((stages, nz)), dma((stages, ny)), dma((stages, ny)),
-            dma((stages,)), dma((stages,)), dma((2,)), dma((2,)),
+            dma((stages,)), dma((stages,)), dma((stages, ny)), dma((stages, ny)),
         ],
         compiler_params=pltpu.CompilerParams(
             collective_id=0, has_side_effects=True, vmem_limit_bytes=48 * 1024 * 1024),

time: 60.6 us -> 55.9 us (0.922)
  Pallas kernels: 57.2 us -> 52.4 us
    pallas_call x1, Pallas kernels: 57.2 us -> 52.4 us  [body(): pl.pallas_call(functools.partial(kernel, n, nsec), out_shape=(jax.ShapeDt...]
where the time goes in v7:
time: 55.9 us; the launch traced here: 55.6 us
  Pallas kernels  52.4 us (94%)
  between operations  1.3 us (2%)
  other arithmetic  1.1 us (2%)
  local copies, waits for them, and re-layouts  0.8 us (1%)
    pallas_call x1, Pallas kernels, body(): pl.pallas_call(functools.partial(kernel, n, nsec), out_shape=(jax.ShapeDt...  52.4 us

profile of v7, /device:TPU:0, one launch (start us, length us, event | category | flops | bytes accessed | tf_op | source)
XLA Modules:
  0.0 55.6 jit_solution(5003347465109294854)
XLA Ops:
  1.3 0.0 copy-start
  1.3 52.4 %shard_map.68 = (bf16[2,4,128,256]{3,2,1,0:T(8,128)(2,1)S(1)}, f32[2,27,16,256]{3,2,1,0:T(8,128)S(1)}) custom-call(s32[1,1]{1,0:T(1,128)S(6)} %copy.9.plan, bf16[1,4,128,256]{3,2,1,0:T(8,128)(2,1)} %incoming.1, bf16[4,4,128,256]{3,2,1,0:T(8,128)(2,1)} %feed.1, bf16[1,2,27,256,256]{4,3,2,1,0:T(8,128)(2,1)} %weights.1), custom_call_target="tpu_custom_call" | custom-call | flops 5435817984 | bytes 7077888 | tf_op jit(solution)/shard_map/pallas_call | solution.py:388
  53.7 0.0 copy-done
  53.7 1.1 %fusion = f32[1,2,27,16,256]{4,3,2,1,0:T(8,128)} fusion(f32[2,27,16,256]{3,2,1,0:T(8,128)S(1)} %get-tuple-element.5, f32[1,2,27,16,256]{4,3,2,1,0:T(8,128)S(1)} %copy-done), kind=kLoop, calls=%fused_computation.1 | loop fusion | flops 663552 | bytes 2654208 | tf_op jit(solution)/shard_map/broadcast_in_dim | solution.py:425
  54.9 0.8 %copy.10 = bf16[2,1,4,128,256]{4,3,2,1,0:T(8,128)(2,1)} copy(bf16[2,1,4,128,256]{4,3,2,1,0:T(8,128)(2,1)S(1)} %bitcast.9) | data formatting | bytes 1048576
Async XLA Ops:
  1.3 52.5 %copy-start = (f32[1,2,27,16,256]{4,3,2,1,0:T(8,128)S(1)}, f32[1,2,27,16,256]{4,3,2,1,0:T(8,128)}, u32[]{:S(2)}) copy-start(f32[1,2,27,16,256]{4,3,2,1,0:T(8,128)} %param.9) | copy-start | bytes 2654212

commit v8 on v7

--- a/solution.py
+++ b/solution.py
@@ -252,11 +252,61 @@
             src_ref=upv.at[0, j], dst_ref=nxt.at[j], send_sem=sec_s.at[j], recv_sem=sec_r.at[j],
             device_id={"section": lax.rem(sec + nsec - 1, nsec)}, device_id_type=MESH)
 
+    stages = 2 * TICKS
+    depth = n * VOX
+
+    lane = lax.broadcasted_iota(jnp.int32, (8, VOX), 1)
+    masks = {}
+    for step, size in ((1, TW), (TW, TH), (PLANE, TD)):
+        at_axis = (lane // step) % size
+        masks[step] = at_axis >= 1
+        masks[-step] = at_axis < size - 1
+
+    def moved(x, by):
+        if by == 0:
+            return x
+        return jnp.where(masks[by], pltpu.roll(x, by % VOX, 2), 0.0)
+
+    def gradient(stage):
+        b = stage % 2
+        d_to_mate(stage, 1 - core).wait_recv()
+        arrive(stage)
+
+        @pl.loop(0, n // 2)
+        def _(r):
+            yy, zz = r // nz, lax.rem(r, nz)
+            for cc in (0, 1):
+                x = d_recv[stage, cc, yy, zz].astype(jnp.float32)
+                x = jnp.where(core == 0, x[:half], x[half:]).reshape(half // 8, 8, VOX)
+                cols = pl.ds(pl.multiple_of((2 * r + cc) * VOX, VOX), VOX)
+                rows = [None] * TAPS
+                for dw in (-1, 0, 1):
+                    xw = moved(x, dw)
+                    for dh in (-1, 0, 1):
+                        xh = moved(xw, dh * TW)
+                        for dd in (-1, 0, 1):
+                            tap = 9 * (dd + 1) + 3 * (dh + 1) + dw + 1
+                            rows[tap] = moved(xh, dd * PLANE).reshape(half, VOX)
+                big[:, cols] = jnp.concatenate(rows, 0).astype(jnp.bfloat16)
+
+        mate_arrives(stage)
+        both = jnp.concatenate([a_recv[stage, 0].reshape(depth, LANES),
+                                a_recv[stage, 1].reshape(depth, LANES)], 1)
+        got = jnp.dot(big[...], both, preferred_element_type=jnp.float32)
+        if stage < 2:
+            acc[b] = got
+        else:
+            grad[1 - b] = (acc[b] + got).reshape(TAPS, half, 2 * LANES)
+
     for tick in range(TICKS):
         if tick == 0:
             cur = first
         else:
             cur = nxt
+            relay_near(1)
+            swap_errors(0)
+            gradient(0)
+            relay_far(1)
             load_pool.wait()
 
             @pl.when(last)
@@ -276,7 +326,7 @@
         fill(eb, ob, dy2)
         if tick == 0:
             loads[1].wait()
-        fwd, bwd = convs(1, lambda: relay_near(1) if tick else None, lambda: relay_far(1) if tick else None)
+        fwd, bwd = convs(1, lambda: None, lambda: None)
         x2 = (cur[1].astype(jnp.float32) - fwd).astype(jnp.bfloat16)
         dx1 = (cur[2].astype(jnp.float32) + bwd * silu_grad(y1, s1)).astype(jnp.bfloat16)
         upv[tick, 1] = x2
@@ -307,56 +357,14 @@
                 sec_copy(3).start()
         pltpu.make_async_copy(upv.at[tick], up.at[tick], up_sem.at[tick]).start()
 
-    lane = lax.broadcasted_iota(jnp.int32, (8, VOX), 1)
-    masks = {}
-    for step, size in ((1, TW), (TW, TH), (PLANE, TD)):
-        at_axis = (lane // step) % size
-        masks[step] = at_axis >= 1
-        masks[-step] = at_axis < size - 1
-
-    def moved(x, by):
-        if by == 0:
-            return x
-        return jnp.where(masks[by], pltpu.roll(x, by % VOX, 2), 0.0)
-
-    stages = 2 * TICKS
-    depth = n * VOX
     relay_near(stages - 1)
-    swap_errors(0)
-    for stage in range(stages):
-        b = stage % 2
-        if stage == 1:
+    swap_errors(1)
+    for stage in range(1, stages):
+        if stage == 2:
             relay_far(stages - 1)
         if stage + 1 < stages:
             swap_errors(stage + 1)
-        d_to_mate(stage, 1 - core).wait_recv()
-        arrive(stage)
-
-        @pl.loop(0, n // 2)
-        def _(r):
-            yy, zz = r // nz, lax.rem(r, nz)
-            for cc in (0, 1):
-                x = d_recv[stage, cc, yy, zz].astype(jnp.float32)
-                x = jnp.where(core == 0, x[:half], x[half:]).reshape(half // 8, 8, VOX)
-                cols = pl.ds(pl.multiple_of((2 * r + cc) * VOX, VOX), VOX)
-                rows = [None] * TAPS
-                for dw in (-1, 0, 1):
-                    xw = moved(x, dw)
-                    for dh in (-1, 0, 1):
-                        xh = moved(xw, dh * TW)
-                        for dd in (-1, 0, 1):
-                            tap = 9 * (dd + 1) + 3 * (dh + 1) + dw + 1
-                            rows[tap] = moved(xh, dd * PLANE).reshape(half, VOX)
-                big[:, cols] = jnp.concatenate(rows, 0).astype(jnp.bfloat16)
-
-        mate_arrives(stage)
-        both = jnp.concatenate([a_recv[stage, 0].reshape(depth, LANES),
-                                a_recv[stage, 1].reshape(depth, LANES)], 1)
-        got = jnp.dot(big[...], both, preferred_element_type=jnp.float32)
-        if stage < 2:
-            acc[b] = got
-        else:
-            grad[1 - b] = (acc[b] + got).reshape(TAPS, half, 2 * LANES)
+        gradient(stage)
 
     @pl.loop(0, stages)
     def _(stage):

time: 55.9 us -> 54.3 us (0.971)
  Pallas kernels: 52.4 us -> 50.9 us
    pallas_call x1, Pallas kernels: 52.4 us -> 50.9 us  [body(): pl.pallas_call(functools.partial(kernel, n, nsec), out_shape=(jax.ShapeDt...]
where the time goes in v8:
time: 54.3 us; the launch traced here: 54.1 us
  Pallas kernels  50.9 us (94%)
  between operations  1.3 us (2%)
  other arithmetic  1.1 us (2%)
  local copies, waits for them, and re-layouts  0.8 us (1%)
    pallas_call x1, Pallas kernels, body(): pl.pallas_call(functools.partial(kernel, n, nsec), out_shape=(jax.ShapeDt...  50.9 us
    broadcast_in_dim x1, other arithmetic, body(): return (up[:, None], new_momentum[None])  1.1 us

profile of v8, /device:TPU:0, one launch (start us, length us, event | category | flops | bytes accessed | tf_op | source)
XLA Modules:
  0.0 54.1 jit_solution(7660839705453829587)
XLA Ops:
  1.3 0.0 copy-start
  1.3 50.9 %shard_map.68 = (bf16[2,4,128,256]{3,2,1,0:T(8,128)(2,1)S(1)}, f32[2,27,16,256]{3,2,1,0:T(8,128)S(1)}) custom-call(s32[1,1]{1,0:T(1,128)S(6)} %copy.9.plan, bf16[1,4,128,256]{3,2,1,0:T(8,128)(2,1)} %incoming.1, bf16[4,4,128,256]{3,2,1,0:T(8,128)(2,1)} %feed.1, bf16[1,2,27,256,256]{4,3,2,1,0:T(8,128)(2,1)} %weights.1), custom_call_target="tpu_custom_call" | custom-call | flops 5435817984 | bytes 7077888 | tf_op jit(solution)/shard_map/pallas_call | solution.py:396
  52.2 0.0 copy-done
  52.2 1.1 %fusion = f32[1,2,27,16,256]{4,3,2,1,0:T(8,128)} fusion(f32[2,27,16,256]{3,2,1,0:T(8,128)S(1)} %get-tuple-element.5, f32[1,2,27,16,256]{4,3,2,1,0:T(8,128)S(1)} %copy-done), kind=kLoop, calls=%fused_computation.1 | loop fusion | flops 663552 | bytes 2654208 | tf_op jit(solution)/shard_map/broadcast_in_dim | solution.py:433
  53.3 0.8 %copy.10 = bf16[2,1,4,128,256]{4,3,2,1,0:T(8,128)(2,1)} copy(bf16[2,1,4,128,256]{4,3,2,1,0:T(8,128)(2,1)S(1)} %bitcast.9) | data formatting | bytes 1048576
Async XLA Ops:
  1.3 50.9 %copy-start = (f32[1,2,27,16,256]{4,3,2,1,0:T(8,128)S(1)}, f32[1,2,27,16,256]{4,3,2,1,0:T(8,128)}, u32[]{:S(2)}) copy-start(f32[1,2,27,16,256]{4,3,2,1,0:T(8,128)} %param.9) | copy-start | bytes 2654212
